TPU v7x, 128 devices: a whole 4x4x4 slice. The times are simulated.
128 devices in a mesh: dp: 4 (over z), expert: 32 (over x, y, core).
Axes of the slice: x: 4, y: 4, z: 4, core: 2. Of those that a mesh axis runs over, the one named last changes fastest.
Arguments:
- layer_input: bfloat16 [16384, 2048], P(('dp', 'expert')), may hold values from -42 to 42
- upstream: bfloat16 [16384, 2048], P(('dp', 'expert')), may hold values from -1.5 to 1.5
- hidden: bfloat16 [16384, 8, 768], P(('dp', 'expert')), may hold values from -6 to 6
- route_ids: int32 [16384, 8], P(('dp', 'expert')), may hold values from 0 to 95, all different within a row; in each aligned block of 128 rows (0 to 127, 128 to 255, ...) at most 16 rows name the same one
- route_prob: float32 [16384, 8], P(('dp', 'expert')), may hold values from 0.05 to 1
- down_weight: bfloat16 [96, 768, 2048], P('expert'), may hold values from -0.21875 to 0.21875
- probe_signs: bfloat16 [96, 768, 2048], P('expert'), may hold values from -1 to 1, as said below
Outputs:
- diag_estimate: float32 [96, 768, 2048], P('expert', None, 'dp')
Inputs may be any that keep to these rules, and one draw needn't show every extreme that they name: `route_ids`: each row names 8 different experts. Among the 128 rows of one device (aligned blocks of rows) no expert is named by more than 16 rows, and in every draw some expert is named by exactly 16 rows of one device. `probe_signs`: every entry is -1 or +1.
All inputs are finite; a program needn't handle non-finite values.
Results may differ from a plain program's by a relative error of at most 0.0045.
Values may be sent and summed in bfloat16 or wider, within the bound.
No kernel may reach another device: no remote copies, remote signals or barrier semaphores. Data moves between devices by JAX's collectives and lax.ppermute only.
A program may use at most 192 MiB of HBM per device.

v0:
```python
import jax
import jax.numpy as jnp
from jax import lax
from jax.sharding import PartitionSpec as P

EPSILON = 1e-06


def slot_places(route_ids, expert_count, capacity):
    flat_ids = route_ids.reshape(-1)
    onehot = (flat_ids[:, None] == jnp.arange(expert_count, dtype=jnp.int32)[None, :]).astype(
        jnp.int32
    )
    earlier = jnp.sum((jnp.cumsum(onehot, axis=0) - onehot) * onehot, axis=1)
    return flat_ids * capacity + earlier


def curvature_tangent(layer_input, upstream, moe_out, moe_tangent):
    summed = layer_input.astype(jnp.float32) + moe_out
    coefficient = upstream.astype(jnp.float32)
    inverse = lax.rsqrt(jnp.mean(summed * summed, axis=-1, keepdims=True) + EPSILON)
    inverse_cube = inverse * inverse * inverse
    upstream_dot = jnp.mean(coefficient * summed, axis=-1, keepdims=True)
    stretch = jnp.mean(summed * moe_tangent, axis=-1, keepdims=True)
    turning = jnp.mean(coefficient * moe_tangent, axis=-1, keepdims=True)
    first = -inverse_cube * stretch * coefficient
    second = (
        3.0 * inverse_cube * inverse * inverse * stretch * upstream_dot - inverse_cube * turning
    ) * summed
    third = inverse_cube * upstream_dot * moe_tangent
    return first + second - third


def shards(layer_input, upstream, hidden, route_ids, route_prob, down_weight, probe_signs):
    token_rows, top_count = route_ids.shape
    local_experts, width_f, width_d = down_weight.shape
    groups = lax.axis_size("expert")
    expert_count = local_experts * groups
    capacity = 3 * token_rows * top_count // (2 * expert_count)
    places = slot_places(route_ids, expert_count, capacity)
    combine = route_prob / jnp.sum(route_prob, axis=1, keepdims=True)
    outgoing = (
        jnp.zeros((expert_count * capacity, width_f), jnp.bfloat16)
        .at[places]
        .set(hidden.reshape(-1, width_f))
    )
    outgoing = outgoing.reshape(groups, local_experts, capacity, width_f)
    arrived = lax.all_to_all(outgoing, "expert", split_axis=0, concat_axis=0, tiled=True)
    primal = jnp.einsum(
        "slcf,lfd->slcd", arrived, down_weight, preferred_element_type=jnp.float32
    ).astype(jnp.bfloat16)
    tangent = jnp.einsum(
        "slcf,lfd->slcd", arrived, probe_signs, preferred_element_type=jnp.float32
    ).astype(jnp.bfloat16)
    primal, tangent = (primal, tangent)
    primal_back, tangent_back = (
        lax.all_to_all(primal, "expert", split_axis=0, concat_axis=0, tiled=True),
        lax.all_to_all(tangent, "expert", split_axis=0, concat_axis=0, tiled=True),
    )
    route_weights = combine[:, :, None]
    primal_rows = primal_back.reshape(-1, width_d)[places].reshape(token_rows, top_count, width_d)
    tangent_rows = tangent_back.reshape(-1, width_d)[places].reshape(token_rows, top_count, width_d)
    moe_out = jnp.sum(route_weights * primal_rows.astype(jnp.float32), axis=1)
    moe_tangent = jnp.sum(route_weights * tangent_rows.astype(jnp.float32), axis=1)
    grad_tangent = curvature_tangent(layer_input, upstream, moe_out, moe_tangent)
    route_grads = (
        (route_weights * grad_tangent[:, None, :]).astype(jnp.bfloat16).reshape(-1, width_d)
    )
    sending = (
        jnp.zeros((expert_count * capacity, width_d), jnp.bfloat16).at[places].set(route_grads)
    )
    sending = sending.reshape(groups, local_experts, capacity, width_d)
    arrived_grads = lax.all_to_all(sending, "expert", split_axis=0, concat_axis=0, tiled=True)
    curvature = jnp.einsum(
        "slcf,slcd->lfd", arrived, arrived_grads, preferred_element_type=jnp.float32
    )
    result = lax.psum_scatter(
        probe_signs.astype(jnp.float32) * curvature, "dp", scatter_dimension=2, tiled=True
    )
    return result


def solution(mesh):
    in_specs = (
        P(("dp", "expert"), None),
        P(("dp", "expert"), None),
        P(("dp", "expert"), None, None),
        P(("dp", "expert"), None),
        P(("dp", "expert"), None),
        P("expert", None, None),
        P("expert", None, None),
    )
    out_specs = P("expert", None, "dp")
    return jax.shard_map(shards, mesh=mesh, in_specs=in_specs, out_specs=out_specs, check_vma=False)
```

profile of v0, /device:TPU:1, one launch (start us, length us, event | category | flops | bytes accessed | tf_op | source)
XLA Modules:
  0.0 573.3 jit_solution(10721275224395148717)
XLA Ops:
  6.5 0.8 broadcast_multiply_fusion
  7.3 0.8 copy.23
  8.3 0.1 copy.22
  8.4 0.1 mul.187
  8.6 27.0 %reduce-window.6 = s32[96,8,128]{2,1,0:T(8,128)S(1)} reduce-window(s32[96,8,128]{2,1,0:T(8,128)S(1)} %fusion.28, s32[]{:T(128)} %constant.10.clone.1), window={size=1x1x128 pad=0_0x0_0x127_0}, to_apply=%region_0.0 | reduce-window | flops 12484608 | bytes 786436 | tf_op jit(solution)/shard_map/reduce-window
  35.6 0.2 slice.12
  35.7 0.2 copy.25
  35.9 0.1 copy.26
  36.0 0.2 broadcast_add_fusion
  36.2 0.1 fusion.27
  36.4 6.9 %scatter_custom_fusion = bf16[1536,768]{1,0:T(8,128)(2,1)} fusion(s32[1024]{0:T(1024)S(1)} %bitcast.67, bf16[128,8,768]{2,1,0:T(8,128)(2,1)S(1)} %copy-done, bf16[]{:T(256)} %constant.8.clone.1), kind=kCustom, calls=%fused_computation.23 | custom fusion | bytes 3932162 | tf_op jit(solution)/shard_map/scatter | solution.py:45
  43.2 40.0 %all_to_all.20 = bf16[32,3,16,768]{3,2,1,0:T(8,128)(2,1)S(1)} all-to-all(bf16[32,3,16,768]{3,2,1,0:T(8,128)(2,1)} %bitcast.63), channel_id=1, replica_groups=mesh['dp'=4,'expert'=32] {'expert'}, dimensions={0} | all-to-all | bytes 4718592 | tf_op jit(solution)/shard_map/all_to_all | solution.py:48
  83.3 1.4 copy-done.2
  84.7 9.1 %convert_bitcast_fusion = bf16[32,3,16,2048]{3,2,0,1:T(8,128)(2,1)S(1)} fusion(bf16[3,768,2048]{2,1,0:T(8,128)(2,1)} %param.13, bf16[32,3,16,768]{3,2,1,0:T(8,128)(2,1)S(1)} %all_to_all.20), kind=kOutput, calls=%fused_computation.15 | convolution fusion | flops 4834983936 | bytes 18087936 | tf_op jit(solution)/shard_map/slcf,lfd->slcd/dot_general | solution.py:52
  93.8 3.2 copy.32
  97.0 4.7 all-to-all-start.2
  101.7 9.3 %convert_bitcast_fusion.1 = bf16[32,3,16,2048]{3,2,0,1:T(8,128)(2,1)S(1)} fusion(bf16[3,768,2048]{2,1,0:T(8,128)(2,1)} %param.12, bf16[32,3,16,768]{3,2,1,0:T(8,128)(2,1)} %copy-done.2), kind=kOutput, calls=%fused_computation.16 | convolution fusion | flops 4834983936 | bytes 18087936 | tf_op jit(solution)/shard_map/slcf,lfd->slcd/dot_general | solution.py:49
  111.0 3.2 copy.30
  114.2 65.3 %all-to-all-done.2 = bf16[32,3,16,2048]{3,2,1,0:T(8,128)(2,1)} async-done(((bf16[32,3,16,2048]{3,2,1,0:T(8,128)(2,1)}), bf16[32,3,16,2048]{3,2,1,0:T(8,128)(2,1)}, u32[]{:S(2)}, u32[]{:S(2)}) %all-to-all-start.2) | async-done | bytes 6291488 | tf_op jit(solution)/shard_map/all_to_all | solution.py:58
  179.6 12.7 %all-to-all-start.1 = ((bf16[32,3,16,2048]{3,2,1,0:T(8,128)(2,1)}), bf16[32,3,16,2048]{3,2,1,0:T(8,128)(2,1)}, u32[]{:S(2)}, u32[]{:S(2)}) async-start(bf16[32,3,16,2048]{3,2,1,0:T(8,128)(2,1)} %copy.30), calls=%async_computation.1 | async-start | bytes 12582912 | tf_op jit(solution)/shard_map/all_to_all | solution.py:57
  192.3 0.1 copy.27
  192.4 0.1 mul.189
  192.5 12.6 %gather_fusion.1 = bf16[1024,2048]{1,0:T(8,128)(2,1)} fusion(bf16[1536,2048]{1,0:T(8,128)(2,1)} %bitcast.14, s32[1024]{0:T(1024)S(1)} %broadcast_clamp_fusion), kind=kCustom, calls=%fused_computation.1 | custom fusion | bytes 8392704 | tf_op jit(solution)/shard_map/gather | solution.py:62
  205.1 65.1 %all-to-all-done.1 = bf16[32,3,16,2048]{3,2,1,0:T(8,128)(2,1)} async-done(((bf16[32,3,16,2048]{3,2,1,0:T(8,128)(2,1)}), bf16[32,3,16,2048]{3,2,1,0:T(8,128)(2,1)}, u32[]{:S(2)}, u32[]{:S(2)}) %all-to-all-start.1) | async-done | bytes 6291488 | tf_op jit(solution)/shard_map/all_to_all | solution.py:57
  270.2 12.4 %gather_fusion = bf16[1024,2048]{1,0:T(8,128)(2,1)} fusion(bf16[1536,2048]{1,0:T(8,128)(2,1)} %bitcast.9, s32[1024]{0:T(1024)S(1)} %broadcast_clamp_fusion), kind=kCustom, calls=%fused_computation | custom fusion | bytes 8392704 | tf_op jit(solution)/shard_map/gather | solution.py:61
  282.6 8.5 %fusion.5 = (f32[128,2048]{1,0:T(8,128)S(1)}, f32[128,2048]{1,0:T(8,128)S(1)}) fusion(bf16[1024,2048]{1,0:T(8,128)(2,1)} %gather_fusion, f32[128,8]{1,0:T(8,128)S(1)} %copy.27, bf16[1024,2048]{1,0:T(8,128)(2,1)} %gather_fusion.1), kind=kLoop, calls=%fused_computation.12 | loop fusion | flops 12058624 | bytes 10489856 | tf_op jit(solution)/shard_map/reduce_sum | solution.py:63
  291.2 0.6 multiply_reduce_fusion
  291.8 0.4 fusion.22
  292.2 10.6 %scatter_custom_fusion.1 = bf16[1536,2048]{1,0:T(8,128)(2,1)} fusion(s32[1024]{0:T(1024)S(1)} %bitcast.69, f32[128,2048]{1,0:T(8,128)S(1)} %fusion.22, f32[1024]{0:T(1024)S(1)} %mul.189, bf16[]{:T(256)} %constant.8.clone.1), kind=kCustom, calls=%fused_computation.17 | custom fusion | flops 4194304 | bytes 7344130 | tf_op jit(solution)/shard_map/scatter | solution.py:70
  302.8 88.2 %all_to_all.21 = bf16[32,3,16,2048]{3,2,1,0:T(8,128)(2,1)S(1)} all-to-all(bf16[32,3,16,2048]{3,2,1,0:T(8,128)(2,1)} %bitcast.62), channel_id=1, replica_groups=mesh['dp'=4,'expert'=32] {'expert'}, dimensions={0} | all-to-all | bytes 12582912 | tf_op jit(solution)/shard_map/all_to_all | solution.py:73
  391.0 11.6 %bitcast_multiply_fusion = f32[3,768,2048]{2,1,0:T(8,128)} fusion(bf16[3,768,2048]{2,1,0:T(8,128)(2,1)} %param.13, bf16[32,3,16,768]{3,2,1,0:T(8,128)(2,1)S(1)} %copy-done.3, bf16[32,3,16,2048]{3,2,1,0:T(8,128)(2,1)S(1)} %all_to_all.21), kind=kOutput, calls=%fused_computation.4 | convolution fusion | flops 4841275392 | bytes 36962304 | tf_op jit(solution)/shard_map/slcf,slcd->lfd/dot_general | solution.py:74
  402.7 163.8 %reduce-scatter.2.cloned.1.call-done = f32[3,768,512]{2,1,0:T(8,128)} async-done(((f32[3,768,2048]{2,1,0:T(8,128)}), f32[3,768,512]{2,1,0:T(8,128)}) %reduce-scatter.2.cloned.1.call-update) | async-done | bytes 4718608 | tf_op jit(solution)/shard_map/reduce_scatter | solution.py:77
  (25 shorter events, 0.4 us)
Async XLA Ops:
  6.5 29.8 %copy-start = (bf16[128,8,768]{2,1,0:T(8,128)(2,1)S(1)}, bf16[128,8,768]{2,1,0:T(8,128)(2,1)}, u32[]{:S(2)}) copy-start(bf16[128,8,768]{2,1,0:T(8,128)(2,1)} %param.9) | copy-start | bytes 4718596
  83.3 1.4 copy-start.2
  97.0 82.6 %all-to-all-start.2 = ((bf16[32,3,16,2048]{3,2,1,0:T(8,128)(2,1)}), bf16[32,3,16,2048]{3,2,1,0:T(8,128)(2,1)}, u32[]{:S(2)}, u32[]{:S(2)}) async-start(bf16[32,3,16,2048]{3,2,1,0:T(8,128)(2,1)} %copy.32), calls=%async_computation.2 | async-start | bytes 12582912 | tf_op jit(solution)/shard_map/all_to_all | solution.py:58
  114.2 78.0 %copy-start.6 = (f32[128,8]{0,1:T(8,128)S(1)}, f32[128,8]{0,1:T(8,128)}, u32[]{:S(2)}) copy-start(f32[128,8]{0,1:T(8,128)} %param.11) | copy-start | bytes 12292
  179.6 90.7 %all-to-all-start.1 = ((bf16[32,3,16,2048]{3,2,1,0:T(8,128)(2,1)}), bf16[32,3,16,2048]{3,2,1,0:T(8,128)(2,1)}, u32[]{:S(2)}, u32[]{:S(2)}) async-start(bf16[32,3,16,2048]{3,2,1,0:T(8,128)(2,1)} %copy.30), calls=%async_computation.1 | async-start | bytes 12582912 | tf_op jit(solution)/shard_map/all_to_all | solution.py:57
  192.2 374.3 %reduce-scatter.2.cloned.1.call-start = ((), (), s32[]{:S(2)}) async-start(), calls=%async_computation.5 | async-start | bytes 23592960 | tf_op jit(solution)/shard_map/reduce_scatter | solution.py:77
  282.6 8.5 %copy-start.4 = (bf16[128,2048]{1,0:T(8,128)(2,1)S(1)}, bf16[128,2048]{1,0:T(8,128)(2,1)}, u32[]{:S(2)}) copy-start(bf16[128,2048]{1,0:T(8,128)(2,1)} %param.8) | copy-start | bytes 1572868
  282.6 8.5 %copy-start.5 = (bf16[128,2048]{1,0:T(8,128)(2,1)S(1)}, bf16[128,2048]{1,0:T(8,128)(2,1)}, u32[]{:S(2)}) copy-start(bf16[128,2048]{1,0:T(8,128)(2,1)} %param.7) | copy-start | bytes 1572868
  302.8 88.2 %copy-start.3 = (bf16[32,3,16,768]{3,2,1,0:T(8,128)(2,1)S(1)}, bf16[32,3,16,768]{3,2,1,0:T(8,128)(2,1)}, u32[]{:S(2)}) copy-start(bf16[32,3,16,768]{3,2,1,0:T(8,128)(2,1)} %copy-done.2) | copy-start | bytes 7077892
  402.6 163.9 %copy-start.1 = (bf16[128,8,768]{2,1,0:T(8,128)(2,1)S(1)}, bf16[128,8,768]{2,1,0:T(8,128)(2,1)}, u32[]{:S(2)}) copy-start(bf16[128,8,768]{2,1,0:T(8,128)(2,1)} %param.9) | copy-start | bytes 4718596
Sparse Core Ops, SparseCore 0:
  402.8 163.6 reduce-scatter.1
where the time goes:
time: 574 us; the launch traced here: 573 us
  waiting for transfers between devices  294 us (51%)
  blocking collectives  128 us (22%)
  other arithmetic  48.3 us (8%)
  local copies, waits for them, and re-layouts  41.6 us (7%)
  matrix products  30 us (5%)
  starting transfers between devices  17.4 us (3%)
  between operations  13.6 us (2%)
    reduce_scatter x1, waiting for transfers between devices, shards(): lax.psum_scatter(probe_signs.astype(jnp.float32) * curvature, 'dp', scatt...  164 us
    all_to_all x1, blocking collectives, shards(): lax.all_to_all(sending, 'expert', split_axis=0, concat_axis=0, tiled=True)  88.2 us
    all_to_all x1, waiting for transfers between devices, shards(): lax.all_to_all(tangent, 'expert', split_axis=0, concat_axis=0, tiled=True)  65.3 us
    all_to_all x1, waiting for transfers between devices, shards(): lax.all_to_all(primal, 'expert', split_axis=0, concat_axis=0, tiled=True)  65.1 us
    all_to_all x1, blocking collectives, shards(): lax.all_to_all(outgoing, 'expert', split_axis=0, concat_axis=0, tiled=True)  40 us
    another operation x3, other arithmetic  27.2 us
    all_to_all x1, starting transfers between devices, shards(): lax.all_to_all(primal, 'expert', split_axis=0, concat_axis=0, tiled=True)  12.7 us
    gather x1, local copies, waits for them, and re-layouts, shards(): tangent_back.reshape(-1, width_d)[places]  12.6 us
  transfers between devices with their start and end apart: 3, of which 3 were waited for; matrix products, arithmetic and copies ran while one was open for 4% of the time, Pallas kernels for 0%

commit v1 on v0

v1 whole, which is shorter than its diff:
```python
import jax
import jax.numpy as jnp
from jax import lax
from jax.experimental import pallas as pl
from jax.experimental.pallas import tpu as pltpu
from jax.sharding import PartitionSpec as P

EPSILON = 1e-06
CAP = 16
VMEM_LIMIT = 56 * 1024 * 1024
F32 = jnp.float32
BF16 = jnp.bfloat16


def params():
    return pltpu.CompilerParams(vmem_limit_bytes=VMEM_LIMIT)


def dot(a, b, dims):
    return lax.dot_general(a, b, (dims, ((), ())), preferred_element_type=F32)


def split_high_low(x):
    high = x.astype(BF16)
    low = (x - high.astype(F32)).astype(BF16)
    return high, low


def place_kernel(ids_ref, comb_ref, hidden_ref, out_ref, sel_ref):
    experts = out_ref.shape[0] // CAP
    routes, tokens = hidden_ref.shape[0], sel_ref.shape[0] // 2
    top = routes // tokens
    ids = ids_ref[...]
    named = lax.broadcasted_iota(jnp.int32, (experts, routes), 0) == ids
    named_f = named.astype(F32)
    before = lax.broadcasted_iota(jnp.int32, (routes, routes), 0) < lax.broadcasted_iota(
        jnp.int32, (routes, routes), 1
    )
    earlier = dot(named_f.astype(BF16), before.astype(F32).astype(BF16), ((1,), (0,)))
    rank = jnp.sum(named_f * earlier, axis=0, keepdims=True)
    place = ids * CAP + rank.astype(jnp.int32)
    owner = lax.broadcasted_iota(jnp.int32, (tokens, routes), 1) // top
    own = owner == lax.broadcasted_iota(jnp.int32, (tokens, routes), 0)
    weights = jnp.where(own, comb_ref[...], 0.0)
    high, low = split_high_low(weights)
    weights = jnp.concatenate([high, low], axis=0)
    hidden = hidden_ref[...]
    step = 512
    for first in range(0, experts * CAP, step):
        slots = lax.broadcasted_iota(jnp.int32, (step, routes), 0) + first
        pick = (slots == place).astype(F32).astype(BF16)
        out_ref[first : first + step, :] = dot(pick, hidden, ((1,), (0,))).astype(BF16)
        sel_ref[:, first : first + step] = dot(weights, pick, ((1,), (1,))).astype(BF16)


def place_routes(ids_row, comb_row, hidden, tokens, experts):
    return pl.pallas_call(
        place_kernel,
        out_shape=(
            jax.ShapeDtypeStruct((experts * CAP, hidden.shape[1]), BF16),
            jax.ShapeDtypeStruct((2 * tokens, experts * CAP), BF16),
        ),
        compiler_params=params(),
    )(ids_row, comb_row, hidden)


def rows_kernel(x_ref, w_ref, out_ref):
    groups, cap, width = x_ref.shape
    x = x_ref[...].reshape(groups * cap, width)
    rows = dot(x, w_ref[0], ((1,), (0,)))
    out_ref[...] = rows.astype(BF16).reshape(groups, cap, -1)


def expert_rows(arrived, weight):
    groups, slots, width_f = arrived.shape
    local, _, width_d = weight.shape
    tile = width_d // 2
    return pl.pallas_call(
        rows_kernel,
        grid=(local, width_d // tile),
        in_specs=[
            pl.BlockSpec((groups, CAP, width_f), lambda l, n: (0, l, 0)),
            pl.BlockSpec((1, width_f, tile), lambda l, n: (l, 0, n)),
        ],
        out_specs=pl.BlockSpec((groups, CAP, tile), lambda l, n: (0, l, n)),
        out_shape=jax.ShapeDtypeStruct((groups, slots, width_d), BF16),
        cost_estimate=pl.CostEstimate(
            flops=2 * groups * slots * width_f * width_d,
            bytes_accessed=2 * (weight.size + arrived.size + groups * slots * width_d),
            transcendentals=0,
        ),
        compiler_params=params(),
    )(arrived, weight)


def token_kernel(sel_ref, primal_ref, tangent_ref, li_ref, up_ref, out_ref, mo_s, mt_s):
    step = pl.program_id(0)
    tokens = li_ref.shape[0]
    tile = primal_ref.shape[1]
    quarters, _, quarter = out_ref.shape
    sel = sel_ref[...]
    mo = dot(sel, primal_ref[...], ((1,), (0,)))
    mt = dot(sel, tangent_ref[...], ((1,), (0,)))
    mo_s[step] = mo[:tokens] + mo[tokens:]
    mt_s[step] = mt[:tokens] + mt[tokens:]

    @pl.when(step == pl.num_programs(0) - 1)
    def _():
        steps = mo_s.shape[0]
        width = steps * tile
        sq = jnp.zeros((tokens, 1), F32)
        dot_us, dot_st, dot_ut = sq, sq, sq
        for n in range(steps):
            cols = slice(n * tile, (n + 1) * tile)
            summed = li_ref[:, cols].astype(F32) + mo_s[n]
            mo_s[n] = summed
            up = up_ref[:, cols].astype(F32)
            mt = mt_s[n]
            sq += jnp.sum(summed * summed, axis=1, keepdims=True)
            dot_us += jnp.sum(up * summed, axis=1, keepdims=True)
            dot_st += jnp.sum(summed * mt, axis=1, keepdims=True)
            dot_ut += jnp.sum(up * mt, axis=1, keepdims=True)
        inverse = lax.rsqrt(sq / width + EPSILON)
        cube = inverse * inverse * inverse
        a, s, u = dot_us / width, dot_st / width, dot_ut / width
        by_up = -cube * s
        by_summed = 3.0 * cube * inverse * inverse * s * a - cube * u
        by_mt = cube * a
        for n in range(steps):
            cols = slice(n * tile, (n + 1) * tile)
            up = up_ref[:, cols].astype(F32)
            grad = by_up * up + by_summed * mo_s[n] - by_mt * mt_s[n]
            part, offset = divmod(n * tile, quarter)
            out_ref[part, :, offset : offset + tile] = grad.astype(BF16)


def token_gradients(sel, primal, tangent, layer_input, upstream, quarters):
    tokens, width = layer_input.shape
    slots = primal.shape[0]
    tile = 256
    steps = width // tile
    return pl.pallas_call(
        token_kernel,
        grid=(steps,),
        in_specs=[
            pl.BlockSpec((2 * tokens, slots), lambda n: (0, 0)),
            pl.BlockSpec((slots, tile), lambda n: (0, n)),
            pl.BlockSpec((slots, tile), lambda n: (0, n)),
            pl.BlockSpec((tokens, width), lambda n: (0, 0)),
            pl.BlockSpec((tokens, width), lambda n: (0, 0)),
        ],
        out_specs=pl.BlockSpec((quarters, tokens, width // quarters), lambda n: (0, 0, 0)),
        out_shape=jax.ShapeDtypeStruct((quarters, tokens, width // quarters), BF16),
        scratch_shapes=[pltpu.VMEM((steps, tokens, tile), F32)] * 2,
        cost_estimate=pl.CostEstimate(
            flops=8 * tokens * slots * width, bytes_accessed=4 * slots * width, transcendentals=0
        ),
        compiler_params=params(),
    )(sel, primal, tangent, layer_input, upstream)


def estimate_kernel(rank_ref, comb_ref, hidden_ref, grad_ref, probe_ref, out_ref, rows_s):
    step = pl.program_id(0)
    groups = grad_ref.shape[0]
    tokens = grad_ref.shape[2]
    local = out_ref.shape[0]
    slot_iota = lax.broadcasted_iota(jnp.int32, (CAP, tokens), 0)

    def pick(i, carry):
        rank = rank_ref[0, i]
        comb = comb_ref[0, i]
        parts = [
            jnp.where(rank[l : l + 1, :] == slot_iota, comb[l : l + 1, :], 0.0) for l in range(local)
        ]
        high, low = split_high_low(jnp.concatenate(parts, axis=0))
        both = dot(jnp.concatenate([high, low], axis=0), grad_ref[i, 0], ((1,), (0,)))
        rows = (both[: local * CAP] + both[local * CAP :]).astype(BF16)
        for l in range(local):
            rows_s[l, pl.ds(pl.multiple_of(i * CAP, CAP), CAP), :] = rows[l * CAP : (l + 1) * CAP]
        return carry

    lax.fori_loop(0, groups, pick, 0, unroll=4)
    for l in range(local):
        hidden = hidden_ref[0, :, l * CAP : (l + 1) * CAP, :].reshape(groups * CAP, -1)
        part = dot(hidden, rows_s[l], ((0,), (0,)))

        @pl.when(step == 0)
        def _():
            out_ref[l] = part

        @pl.when(step > 0)
        def _():
            out_ref[l] += part

        @pl.when(step == pl.num_programs(0) - 1)
        def _():
            out_ref[l] = out_ref[l] * probe_ref[l].astype(F32)


def estimate(rank, comb, hidden, grads, probe):
    parts, groups, slots, width_f = hidden.shape
    tokens, quarter = grads.shape[2:]
    local = probe.shape[0]
    return pl.pallas_call(
        estimate_kernel,
        grid=(parts,),
        in_specs=[
            pl.BlockSpec((1, groups, local, tokens), lambda g: (g, 0, 0, 0)),
            pl.BlockSpec((1, groups, local, tokens), lambda g: (g, 0, 0, 0)),
            pl.BlockSpec((1, groups, slots, width_f), lambda g: (g, 0, 0, 0)),
            pl.BlockSpec((groups, 1, tokens, quarter), lambda g: (0, g, 0, 0)),
            pl.BlockSpec((local, width_f, quarter), lambda g: (0, 0, 0)),
        ],
        out_specs=pl.BlockSpec((local, width_f, quarter), lambda g: (0, 0, 0)),
        out_shape=jax.ShapeDtypeStruct((local, width_f, quarter), F32),
        scratch_shapes=[pltpu.VMEM((local, groups * CAP, quarter), BF16)],
        cost_estimate=pl.CostEstimate(
            flops=2 * parts * groups * slots * width_f * quarter,
            bytes_accessed=2 * (hidden.size + grads.size) + 6 * local * width_f * quarter,
            transcendentals=0,
        ),
        compiler_params=params(),
    )(rank, comb, hidden, grads, probe)


def local_routes(ids, comb, first, local):
    tokens = ids.shape[-1]
    own = first + jnp.arange(local, dtype=jnp.int32)
    match = ids[..., None, :, :] == own[:, None, None]
    named = jnp.any(match, axis=-2)
    weight = jnp.sum(jnp.where(match, comb[..., None, :, :], 0.0), axis=-2)
    before = jnp.triu(jnp.ones((tokens, tokens), F32), 1).astype(BF16)
    earlier = jnp.einsum(
        "gslt,tu->gslu", named.astype(BF16), before, preferred_element_type=F32
    ).astype(jnp.int32)
    return jnp.where(named, earlier, -1), weight


def shards(layer_input, upstream, hidden, route_ids, route_prob, down_weight, probe_signs):
    tokens, top = route_ids.shape
    local, width_f, width_d = down_weight.shape
    groups, parts = lax.axis_size("expert"), lax.axis_size("dp")
    experts = local * groups
    quarter = width_d // parts
    combine = route_prob / jnp.sum(route_prob, axis=1, keepdims=True)
    ids_t, comb_t = route_ids.T, combine.T
    outgoing, sel = place_routes(
        route_ids.reshape(1, -1), combine.reshape(1, -1), hidden.reshape(-1, width_f), tokens, experts
    )
    arrived = lax.all_to_all(
        outgoing.reshape(groups, local * CAP, width_f), "expert", 0, 0, tiled=True
    )
    ids_all = lax.all_gather(ids_t, ("dp", "expert"), axis=0, tiled=False)
    comb_all = lax.all_gather(comb_t, ("dp", "expert"), axis=0, tiled=False)
    hidden_all = lax.all_gather(arrived, "dp", axis=0, tiled=False)
    tangent = lax.all_to_all(expert_rows(arrived, probe_signs), "expert", 0, 0, tiled=True)
    primal = lax.all_to_all(expert_rows(arrived, down_weight), "expert", 0, 0, tiled=True)
    grads = token_gradients(
        sel,
        primal.reshape(-1, width_d),
        tangent.reshape(-1, width_d),
        layer_input,
        upstream,
        parts,
    )
    grads = lax.all_to_all(grads, "dp", 0, 0, tiled=True)
    grads_all = lax.all_gather(grads, "expert", axis=0, tiled=False)
    rank, comb = local_routes(
        ids_all.reshape(parts, groups, top, tokens),
        comb_all.reshape(parts, groups, top, tokens),
        lax.axis_index("expert") * local,
        local,
    )
    probe = lax.dynamic_slice_in_dim(probe_signs, lax.axis_index("dp") * quarter, quarter, 2)
    return estimate(rank, comb, hidden_all, grads_all, probe)


def solution(mesh):
    in_specs = (
        P(("dp", "expert"), None),
        P(("dp", "expert"), None),
        P(("dp", "expert"), None, None),
        P(("dp", "expert"), None),
        P(("dp", "expert"), None),
        P("expert", None, None),
        P("expert", None, None),
    )
    out_specs = P("expert", None, "dp")
    return jax.shard_map(shards, mesh=mesh, in_specs=in_specs, out_specs=out_specs, check_vma=False)
```

time: 574 us -> 370 us (0.64)
  waiting for transfers between devices: 294 us -> 66.6 us
  blocking collectives: 128 us -> 210 us
  Pallas kernels: 0 us -> 64.2 us
  other arithmetic: 48.3 us -> 4.55 us
  local copies, waits for them, and re-layouts: 41.6 us -> 5.61 us
  matrix products: 30 us -> 0.16 us
  starting transfers between devices: 17.4 us -> 4.76 us
    reduce_scatter x1 -> x0, waiting for transfers between devices: 164 us -> none  [shards(): lax.psum_scatter(probe_signs.astype(jnp.float32) * curvature, 'dp', scatt...]
    all_gather x0 -> x2, blocking collectives: none -> 69.2 us  [the longest x1 34.7 us: shards(): comb_all = lax.all_gather(comb_t, ('dp', 'expert'), axis=0, tiled=False)]
    pallas_call x0 -> x5, Pallas kernels: none -> 64.2 us  [the longest x1 23.4 us: estimate(): pl.pallas_call(estimate_kernel, grid=(parts,), in_specs=[pl.BlockSpec((1,...]
    all_to_all x2 -> x1, waiting for transfers between devices: 130 us -> 66.6 us  [shards(): lax.all_to_all(expert_rows(arrived, probe_signs), 'expert', 0, 0, tiled=T...]
    dot_general x3 -> x1, matrix products: 30 us -> 0.16 us  [local_routes(): jnp.einsum('gslt,tu->gslu', named.astype(BF16), before, preferred_element...]
    another operation x3 -> x0, other arithmetic: 27.2 us -> none
    gather x2 -> x0, local copies, waits for them, and re-layouts: 25 us -> none  [the longest x1 12.6 us: shards(): tangent_back.reshape(-1, width_d)[places]]
    all_to_all x2 -> x1, starting transfers between devices: 17.4 us -> 4.71 us  [shards(): lax.all_to_all(expert_rows(arrived, probe_signs), 'expert', 0, 0, tiled=T...]
  transfers between devices with their start and end apart: 3 -> 3, of which waited for: 3 -> 1; matrix products, arithmetic and copies ran while one was open for 4% -> 2% of each run, Pallas kernels for 0% -> 9%
where the time goes in v1:
time: 370 us; the launch traced here: 369 us
  blocking collectives  210 us (57%)
  waiting for transfers between devices  66.6 us (18%)
  Pallas kernels  64.2 us (17%)
  between operations  13.5 us (4%)
  local copies, waits for them, and re-layouts  5.61 us (2%)
  starting transfers between devices  4.76 us (1%)
  other arithmetic  4.55 us (1%)
    all_to_all x1, blocking collectives, shards(): lax.all_to_all(expert_rows(arrived, down_weight), 'expert', 0, 0, tiled=T...  85.8 us
    all_to_all x1, waiting for transfers between devices, shards(): lax.all_to_all(expert_rows(arrived, probe_signs), 'expert', 0, 0, tiled=T...  66.6 us
    all_to_all x1, blocking collectives, shards(): lax.all_to_all(outgoing.reshape(groups, local * CAP, width_f), 'expert',...  40.1 us
    all_gather x1, blocking collectives, shards(): comb_all = lax.all_gather(comb_t, ('dp', 'expert'), axis=0, tiled=False)  34.7 us
    all_gather x1, blocking collectives, shards(): ids_all = lax.all_gather(ids_t, ('dp', 'expert'), axis=0, tiled=False)  34.5 us
    pallas_call x1, Pallas kernels, estimate(): pl.pallas_call(estimate_kernel, grid=(parts,), in_specs=[pl.BlockSpec((1,...  23.4 us
    pallas_call x2, Pallas kernels, expert_rows(): pl.pallas_call(rows_kernel, grid=(local, width_d // tile), in_specs=[pl.B...  22.7 us
    all_to_all x1, blocking collectives, shards(): grads = lax.all_to_all(grads, 'dp', 0, 0, tiled=True)  14.4 us
  transfers between devices with their start and end apart: 3, of which 1 were waited for; matrix products, arithmetic and copies ran while one was open for 2% of the time, Pallas kernels for 9%

profile of v1, /device:TPU:1, one launch (start us, length us, event | category | flops | bytes accessed | tf_op | source)
XLA Modules:
  0.0 368.8 jit_solution(18363107049382473091)
XLA Ops:
  6.5 0.0 all-gather.7.cloned.1.call-start
  6.5 0.7 reduce_sum.18
  7.2 0.7 broadcast_divide_fusion
  7.9 0.1 copy.23
  8.0 0.7 reshape.26.comb_ref
  8.7 0.8 copy.22
  9.5 0.7 reshape.25.ids_ref
  10.2 6.9 %shard_map.73 = (bf16[1536,768]{1,0:T(8,128)(2,1)}, bf16[256,1536]{1,0:T(8,128)(2,1)}) custom-call(s32[1,1024]{1,0:T(1,128)} %reshape.25.ids_ref, f32[1,1024]{1,0:T(1,128)} %reshape.26.comb_ref, bf16[1024,768]{1,0:T(8,128)(2,1)} %bitcast.23), custom_call_target="tpu_custom_call" | custom-call | tf_op jit(solution)/shard_map/pallas_call | solution.py:57
  17.1 40.1 %all_to_all.20.x_ref = bf16[32,48,768]{2,1,0:T(8,128)(2,1)} all-to-all(bf16[32,48,768]{2,1,0:T(8,128)(2,1)} %bitcast.21), channel_id=1, replica_groups=mesh['dp'=4,'expert'=32] {'expert'}, dimensions={0} | all-to-all | bytes 4718592 | tf_op jit(solution)/shard_map/all_to_all | solution.py:250
  57.3 0.0 all-gather.7.cloned.1.call-update
  57.3 11.5 %shard_map.75 = bf16[32,48,2048]{2,1,0:T(8,128)(2,1)} custom-call(bf16[32,48,768]{2,1,0:T(8,128)(2,1)} %all_to_all.20.x_ref, bf16[3,768,2048]{2,1,0:T(8,128)(2,1)} %w_ref.3), custom_call_target="tpu_custom_call" | custom-call | flops 4831838208 | bytes 18087936 | tf_op jit(solution)/shard_map/pallas_call | solution.py:78
  68.8 4.7 %all-to-all-start.2 = ((bf16[32,48,2048]{2,1,0:T(8,128)(2,1)}), bf16[32,48,2048]{2,1,0:T(8,128)(2,1)}, u32[]{:S(2)}, u32[]{:S(2)}) async-start(bf16[32,48,2048]{2,1,0:T(8,128)(2,1)} %shard_map.75), calls=%async_computation.2 | async-start | bytes 12582912 | tf_op jit(solution)/shard_map/all_to_all | solution.py:256
  73.5 0.0 all-gather.9.cloned.1.call-start
  73.6 11.2 %shard_map.74 = bf16[32,48,2048]{2,1,0:T(8,128)(2,1)} custom-call(bf16[32,48,768]{2,1,0:T(8,128)(2,1)} %all_to_all.20.x_ref, bf16[3,768,2048]{2,1,0:T(8,128)(2,1)} %w_ref.2), custom_call_target="tpu_custom_call" | custom-call | flops 4831838208 | bytes 18087936 | tf_op jit(solution)/shard_map/pallas_call | solution.py:78
  84.8 66.6 %all-to-all-done.2 = bf16[32,48,2048]{2,1,0:T(8,128)(2,1)} async-done(((bf16[32,48,2048]{2,1,0:T(8,128)(2,1)}), bf16[32,48,2048]{2,1,0:T(8,128)(2,1)}, u32[]{:S(2)}, u32[]{:S(2)}) %all-to-all-start.2) | async-done | bytes 6291488 | tf_op jit(solution)/shard_map/all_to_all | solution.py:256
  151.4 85.8 %all_to_all.21 = bf16[32,48,2048]{2,1,0:T(8,128)(2,1)} all-to-all(bf16[32,48,2048]{2,1,0:T(8,128)(2,1)} %shard_map.74), channel_id=1, replica_groups=mesh['dp'=4,'expert'=32] {'expert'}, dimensions={0} | all-to-all | bytes 12582912 | tf_op jit(solution)/shard_map/all_to_all | solution.py:257
  237.2 0.0 copy-start.1
  237.2 11.1 %shard_map.76 = bf16[4,128,512]{2,1,0:T(8,128)(2,1)} custom-call(bf16[256,1536]{1,0:T(8,128)(2,1)} %get-tuple-element.8.sel_ref, bf16[1536,2048]{1,0:T(8,128)(2,1)} %bitcast.16, bf16[1536,2048]{1,0:T(8,128)(2,1)} %bitcast.10.tangent_ref, bf16[128,2048]{1,0:T(8,128)(2,1)} %li_ref.1, bf16[128,2048]{1,0:T(8,128)(2,1)} %up_ref.1), custom_call_target="tpu_custom_call" | custom-call | flops 3221225472 | bytes 12582912 | tf_op jit(solution)/shard_map/pallas_call | solution.py:142
  248.3 14.4 %all_to_all.22 = bf16[4,128,512]{2,1,0:T(8,128)(2,1)} all-to-all(bf16[4,128,512]{2,1,0:T(8,128)(2,1)} %shard_map.76), channel_id=1, replica_groups=mesh['dp'=4,'expert'=32] {'dp'}, dimensions={0} | all-to-all | bytes 1048576 | tf_op jit(solution)/shard_map/all_to_all | solution.py:266
  262.7 0.0 all-gather.9.cloned.1.call-update
  262.7 0.0 copy-done.1
  262.7 34.5 %all-gather = s32[1024,128]{1,0:T(8,128)S(1)} all-gather(s32[8,128]{1,0:T(8,128)S(1)} %bitcast.24), channel_id=2, replica_groups=mesh['dp'=4,'expert'=32] {'dp','expert'}, dimensions={0}, use_global_device_ids=true | all-gather | bytes 528384 | tf_op jit(solution)/shard_map/all_gather | solution.py:253
  297.2 0.7 compare_reduce_fusion
  297.9 0.0 copy-start
  297.9 3.3 constant_dynamic-slice_fusion.probe_ref
  301.3 0.0 copy-done
  301.3 34.7 %all-gather.1 = f32[1024,128]{1,0:T(8,128)S(1)} all-gather(f32[8,128]{1,0:T(8,128)S(1)} %fusion.10), channel_id=3, replica_groups=mesh['dp'=4,'expert'=32] {'dp','expert'}, dimensions={0}, use_global_device_ids=true | all-gather | bytes 528384 | tf_op jit(solution)/shard_map/all_gather | solution.py:254
  336.0 1.5 fusion.comb_ref
  337.5 0.2 fusion.2
  337.6 0.9 fusion.1.rank_ref
  338.5 0.0 all-gather.9.cloned.1.call-done
  338.5 23.4 %shard_map.77 = f32[3,768,512]{2,1,0:T(8,128)} custom-call(s32[4,32,3,128]{3,2,1,0:T(4,128)} %fusion.1.rank_ref, f32[4,32,3,128]{3,2,1,0:T(4,128)} %fusion.comb_ref, bf16[4,32,48,768]{3,2,1,0:T(8,128)(2,1)} %bitcast.18, bf16[32,4,128,512]{3,2,1,0:T(8,128)(2,1)} %bitcast.17, bf16[3,768,512]{2,1,0:T(8,128)(2,1)} %constant_dynamic-slice_fusion.probe_ref), custom_call_target="tpu_custom_call" | custom-call | flops 4831838208 | bytes 33292288 | tf_op jit(solution)/shard_map/pallas_call | solution.py:204
  (3 shorter events, 0.0 us)
Async XLA Ops:
  6.5 332.0 %all-gather.7.cloned.1.call-start = ((), (), s32[]{:S(2)}) async-start(), calls=%async_computation.4 | async-start | bytes 11796480 | tf_op jit(solution)/shard_map/all_gather | solution.py:255
  68.8 82.6 %all-to-all-start.2 = ((bf16[32,48,2048]{2,1,0:T(8,128)(2,1)}), bf16[32,48,2048]{2,1,0:T(8,128)(2,1)}, u32[]{:S(2)}, u32[]{:S(2)}) async-start(bf16[32,48,2048]{2,1,0:T(8,128)(2,1)} %shard_map.75), calls=%async_computation.2 | async-start | bytes 12582912 | tf_op jit(solution)/shard_map/all_to_all | solution.py:256
  73.5 265.0 %all-gather.9.cloned.1.call-start = ((), (), s32[]{:S(2)}) async-start(), calls=%async_computation.5 | async-start | bytes 17301504 | tf_op jit(solution)/shard_map/all_gather | solution.py:267
  237.2 25.5 %copy-start.1 = (s32[128,8]{0,1:T(8,128)S(1)}, s32[128,8]{0,1:T(8,128)}, u32[]{:S(2)}) copy-start(s32[128,8]{0,1:T(8,128)} %param.10) | copy-start | bytes 12292
  297.9 3.3 copy-start
Sparse Core Ops, SparseCore 0:
  57.4 90.3 all-gather.6
  262.8 69.4 all-gather.8

commit v2 on v0

v2 whole, which is shorter than its diff:
```python
import jax
import jax.numpy as jnp
from jax import lax
from jax.experimental import pallas as pl
from jax.experimental.pallas import tpu as pltpu
from jax.sharding import PartitionSpec as P

EPSILON = 1e-06
CAP = 16
SIDE = 4
CORES = 2
FACTS = 128
VMEM_LIMIT = 56 * 1024 * 1024
F32 = jnp.float32
BF16 = jnp.bfloat16


def params():
    return pltpu.CompilerParams(vmem_limit_bytes=VMEM_LIMIT)


def dot(a, b, dims):
    return lax.dot_general(a, b, (dims, ((), ())), preferred_element_type=F32)


def device_at(x, y, core):
    return (x * SIDE + y) * CORES + core


def shift(value, dx, dy, core):
    pairs = []
    for i in range(SIDE * SIDE * CORES):
        x, y, c = i // (SIDE * CORES), i // CORES % SIDE, i % CORES
        pairs.append((i, device_at((x + dx) % SIDE, (y + dy) % SIDE, c ^ core)))
    return lax.ppermute(value, "expert", pairs)


def place_kernel(ids_ref, hidden_ref, facts_ref, out_ref):
    experts = out_ref.shape[0] // CAP
    routes = hidden_ref.shape[0]
    ids = ids_ref[...]
    named = (lax.broadcasted_iota(jnp.int32, (experts, routes), 0) == ids).astype(F32)
    before = lax.broadcasted_iota(jnp.int32, (routes, routes), 0) < lax.broadcasted_iota(
        jnp.int32, (routes, routes), 1
    )
    earlier = dot(named.astype(BF16), before.astype(F32).astype(BF16), ((1,), (0,)))
    rank = jnp.sum(named * earlier, axis=0, keepdims=True)
    place = ids * CAP + rank.astype(jnp.int32)
    hidden, facts = hidden_ref[...], facts_ref[...]
    width = hidden.shape[1]
    step = 512
    for first in range(0, experts * CAP, step):
        slots = lax.broadcasted_iota(jnp.int32, (step, routes), 0) + first
        pick = (slots == place).astype(F32).astype(BF16)
        out_ref[first : first + step, :width] = dot(pick, hidden, ((1,), (0,))).astype(BF16)
        out_ref[first : first + step, width:] = dot(pick, facts, ((1,), (0,))).astype(BF16)


def place_routes(ids_row, hidden, facts, experts):
    return pl.pallas_call(
        place_kernel,
        out_shape=jax.ShapeDtypeStruct((experts * CAP, hidden.shape[1] + FACTS), BF16),
        compiler_params=params(),
    )(ids_row, hidden, facts)


def rows_kernel(order_ref, x_ref, w_ref, *refs):
    *out_refs, x_s = refs
    groups, cap, width = x_ref.shape
    for j in range(groups):
        x_s[j * cap : (j + 1) * cap, :] = x_ref[order_ref[j]]
    width_f, width_d = w_ref.shape[1:]
    each = groups // len(out_refs)
    tile = 1024
    for n in range(0, width_d, tile):
        rows = dot(x_s[:, :width_f], w_ref[0, :, n : n + tile], ((1,), (0,))).astype(BF16)
        for j, out_ref in enumerate(out_refs):
            part = rows[j * each * cap : (j + 1) * each * cap]
            out_ref[:, :, n : n + tile] = part.reshape(each, cap, tile)
    for j, out_ref in enumerate(out_refs):
        part = x_s[j * each * cap : (j + 1) * each * cap, width_f:]
        out_ref[:, :, width_d:] = part.reshape(each, cap, FACTS)


def expert_rows(order, arrived, weight, outs):
    groups, slots, width_x = arrived.shape
    local, width_f, width_d = weight.shape
    each = groups // outs
    width = width_d + FACTS
    spec = pl.BlockSpec((each, CAP, width), lambda l, order: (0, l, 0))
    return pl.pallas_call(
        rows_kernel,
        grid_spec=pltpu.PrefetchScalarGridSpec(
            num_scalar_prefetch=1,
            grid=(local,),
            in_specs=[
                pl.BlockSpec((groups, CAP, width_x), lambda l, order: (0, l, 0)),
                pl.BlockSpec((1, width_f, width_d), lambda l, order: (l, 0, 0)),
            ],
            out_specs=[spec] * outs,
            scratch_shapes=[pltpu.VMEM((groups * CAP, width_x), BF16)],
        ),
        out_shape=[jax.ShapeDtypeStruct((each, slots, width), BF16)] * outs,
        cost_estimate=pl.CostEstimate(
            flops=2 * groups * slots * width_f * width_d,
            bytes_accessed=2 * (weight.size + arrived.size + groups * slots * width),
            transcendentals=0,
        ),
        compiler_params=params(),
    )(order, arrived, weight)


def selection(facts, tokens):
    here = lax.broadcasted_iota(jnp.int32, (facts.shape[0], tokens), 1).astype(F32)
    facts = facts.astype(F32)
    mine = here == facts[:, 0:1]
    high = jnp.where(mine, facts[:, 1:2], 0.0).astype(BF16)
    low = jnp.where(mine, facts[:, 2:3], 0.0).astype(BF16)
    return high, low


def middle_kernel(*refs):
    sel_s = refs[-1]
    owners, tokens = sel_s.shape[0], sel_s.shape[2] // 2
    outs = 1 if len(refs) == 4 else owners
    count = (len(refs) - outs - 1) // 2
    row_refs, facts_refs = refs[:count], refs[count : 2 * count]
    out_refs = refs[2 * count : -1]

    def of_owner(blocks, o):
        if len(blocks) == 1:
            return blocks[0][:, o].reshape(-1, blocks[0].shape[-1])
        return jnp.concatenate([ref[o] for ref in blocks], axis=0)

    @pl.when(pl.program_id(0) == 0)
    def _():
        for o in range(owners):
            high, low = selection(of_owner(facts_refs, o), tokens)
            sel_s[o, :, :tokens] = high
            sel_s[o, :, tokens:] = low

    for o in range(owners):
        both = dot(sel_s[o], of_owner(row_refs, o), ((0,), (0,)))
        total = both[:tokens] + both[tokens:]
        if outs == 1:
            out_refs[0][o] = total.astype(out_refs[0].dtype)
        else:
            out_refs[o][...] = total.astype(out_refs[o].dtype)


def middle_sums(rows, tokens):
    owners = SIDE
    slots, width = rows[0].shape[-2:]
    width -= FACTS
    tile = 512
    if len(rows) == 1:
        sources = rows[0].shape[0]
        row_specs = [pl.BlockSpec((sources, owners, slots, tile), lambda n: (0, 0, 0, n))]
        facts_specs = [
            pl.BlockSpec((sources, owners, slots, FACTS), lambda n: (0, 0, 0, width // FACTS))
        ]
        out_specs = [pl.BlockSpec((owners, tokens, tile), lambda n: (0, 0, n))]
        out_shape = [jax.ShapeDtypeStruct((owners, tokens, width), BF16)]
    else:
        sources = len(rows)
        row_specs = [pl.BlockSpec((owners, slots, tile), lambda n: (0, 0, n))] * sources
        facts_specs = [
            pl.BlockSpec((owners, slots, FACTS), lambda n: (0, 0, width // FACTS))
        ] * sources
        out_specs = [pl.BlockSpec((tokens, tile), lambda n: (0, n))] * owners
        out_shape = [jax.ShapeDtypeStruct((tokens, width), F32)]
        out_shape += [jax.ShapeDtypeStruct((tokens, width), BF16)] * (owners - 1)
    return pl.pallas_call(
        middle_kernel,
        grid=(width // tile,),
        in_specs=row_specs + facts_specs,
        out_specs=out_specs,
        out_shape=out_shape,
        scratch_shapes=[pltpu.VMEM((owners, sources * slots, 2 * tokens), BF16)],
        cost_estimate=pl.CostEstimate(
            flops=4 * owners * sources * slots * tokens * width,
            bytes_accessed=2 * owners * sources * slots * width,
            transcendentals=0,
        ),
        compiler_params=params(),
    )(*rows, *rows)


def token_kernel(part_ref, *refs):
    primal, tangent = refs[:SIDE], refs[SIDE]
    li_ref, up_ref = refs[SIDE + 1 : SIDE + 3]
    out_refs, grad_s = refs[SIDE + 3 : -1], refs[-1]
    summed = li_ref[...].astype(F32)
    for ref in primal:
        summed += ref[...].astype(F32)
    mt = tangent[0].astype(F32)
    for i in range(1, SIDE):
        mt += tangent[i].astype(F32)
    up = up_ref[...].astype(F32)
    width = up.shape[1]
    inverse = lax.rsqrt(jnp.sum(summed * summed, axis=1, keepdims=True) / width + EPSILON)
    cube = inverse * inverse * inverse
    a = jnp.sum(up * summed, axis=1, keepdims=True) / width
    s = jnp.sum(summed * mt, axis=1, keepdims=True) / width
    u = jnp.sum(up * mt, axis=1, keepdims=True) / width
    by_summed = 3.0 * cube * inverse * inverse * s * a - cube * u
    grad = (-cube * s) * up + by_summed * summed - (cube * a) * mt
    parts = len(out_refs)
    quarter = width // parts
    for p in range(parts):
        grad_s[p] = grad[:, p * quarter : (p + 1) * quarter].astype(BF16)
    for p in range(parts):
        out_refs[p][...] = grad_s[(part_ref[0] + p) % parts]


def token_gradients(part, primal, tangent, layer_input, upstream, parts):
    tokens, width = layer_input.shape
    tile = 16
    quarter = width // parts
    spec = pl.BlockSpec((tile, width), lambda n, part: (n, 0))
    return pl.pallas_call(
        token_kernel,
        grid_spec=pltpu.PrefetchScalarGridSpec(
            num_scalar_prefetch=1,
            grid=(tokens // tile,),
            in_specs=[spec] * SIDE
            + [pl.BlockSpec((SIDE, tile, width), lambda n, part: (0, n, 0)), spec, spec],
            out_specs=[pl.BlockSpec((tile, quarter), lambda n, part: (n, 0))] * parts,
            scratch_shapes=[pltpu.VMEM((parts, tile, quarter), BF16)],
        ),
        out_shape=[jax.ShapeDtypeStruct((tokens, quarter), BF16)] * parts,
        compiler_params=params(),
    )(part, *primal, tangent, layer_input, upstream)


def turn_kernel(hidden_ref, out_ref):
    _, groups, cap, width = hidden_ref.shape
    out_ref[0, 0] = hidden_ref[0].reshape(groups * cap, width)[:, : out_ref.shape[2]].T


def turned(hidden, local):
    parts, groups, slots, width_x = hidden.shape
    width = width_x - FACTS
    return pl.pallas_call(
        turn_kernel,
        grid=(parts, local),
        in_specs=[pl.BlockSpec((1, groups, CAP, width_x), lambda g, l: (g, 0, l, 0))],
        out_specs=pl.BlockSpec((1, 1, width, groups * CAP), lambda g, l: (g, l, 0, 0)),
        out_shape=jax.ShapeDtypeStruct((parts, local, width, groups * CAP), BF16),
        cost_estimate=pl.CostEstimate(
            flops=0, bytes_accessed=4 * hidden.size, transcendentals=0
        ),
        compiler_params=params(),
    )(hidden)


def estimate_kernel(part_ref, facts_ref, hidden_ref, grad_ref, probe_ref, out_ref, rows_s):
    step = pl.program_id(0)
    groups, _, tokens, quarter = grad_ref.shape
    local = out_ref.shape[0]
    slots = local * CAP
    nothing = jnp.zeros((slots, tokens), BF16)
    for i in range(0, groups, 2):
        high0, low0 = selection(facts_ref[0, i], tokens)
        high1, low1 = selection(facts_ref[0, i + 1], tokens)
        first = jnp.concatenate([high0, nothing, low0, nothing], axis=0)
        second = jnp.concatenate([nothing, high1, nothing, low1], axis=0)
        sel = jnp.concatenate([first, second], axis=1)
        grads = grad_ref[i : i + 2, 0].reshape(2 * tokens, quarter)
        both = dot(sel, grads, ((1,), (0,)))
        rows = (both[: 2 * slots] + both[2 * slots :]).astype(BF16)
        for j in range(2):
            for l in range(local):
                start = j * slots + l * CAP
                rows_s[l, (i + j) * CAP : (i + j + 1) * CAP, :] = rows[start : start + CAP]
    for l in range(local):
        part = dot(hidden_ref[0, l], rows_s[l], ((1,), (0,)))

        @pl.when(step == 0)
        def _():
            out_ref[l] = part

        @pl.when(jnp.logical_and(step > 0, step < pl.num_programs(0) - 1))
        def _():
            out_ref[l] += part

        @pl.when(step == pl.num_programs(0) - 1)
        def _():
            out_ref[l] = (out_ref[l] + part) * probe_ref[l].astype(F32)


def estimate(part, arrived, hidden, grads, probe):
    parts, local, width_f, slots = hidden.shape
    groups, _, tokens, quarter = grads.shape

    def group(s, part):
        return (part[0] + parts - s) % parts

    return pl.pallas_call(
        estimate_kernel,
        grid_spec=pltpu.PrefetchScalarGridSpec(
            num_scalar_prefetch=1,
            grid=(parts,),
            in_specs=[
                pl.BlockSpec(
                    (1, groups, local * CAP, FACTS), lambda s, p: (group(s, p), 0, 0, width_f // FACTS)
                ),
                pl.BlockSpec((1, local, width_f, slots), lambda s, p: (group(s, p), 0, 0, 0)),
                pl.BlockSpec((groups, 1, tokens, quarter), lambda s, p: (0, s, 0, 0)),
                pl.BlockSpec((local, width_f, quarter), lambda s, p: (0, 0, p[0])),
            ],
            out_specs=pl.BlockSpec((local, width_f, quarter), lambda s, p: (0, 0, 0)),
            scratch_shapes=[pltpu.VMEM((local, slots, quarter), BF16)],
        ),
        out_shape=jax.ShapeDtypeStruct((local, width_f, quarter), F32),
        cost_estimate=pl.CostEstimate(
            flops=2 * parts * slots * local * width_f * quarter,
            bytes_accessed=2 * (hidden.size + grads.size) + 6 * local * width_f * quarter,
            transcendentals=0,
        ),
        compiler_params=params(),
    )(part, arrived, hidden, grads, probe)


def shards(layer_input, upstream, hidden, route_ids, route_prob, down_weight, probe_signs):
    tokens, top = route_ids.shape
    local, width_f, width_d = down_weight.shape
    groups, parts = lax.axis_size("expert"), lax.axis_size("dp")
    experts = local * groups
    me, part = lax.axis_index("expert"), lax.axis_index("dp")
    x, y, core = me // (SIDE * CORES), me // CORES % SIDE, me % CORES
    side, cores = jnp.arange(SIDE, dtype=jnp.int32), jnp.arange(CORES, dtype=jnp.int32)

    combine = route_prob / jnp.sum(route_prob, axis=1, keepdims=True)
    flat = combine.reshape(-1)
    high = lax.reduce_precision(flat, 8, 7)
    high, low = high.astype(BF16), (flat - high).astype(BF16)
    owner = (jnp.arange(tokens * top, dtype=jnp.int32) // top).astype(BF16)
    facts = jnp.pad(jnp.stack([owner, high, low], axis=1), ((0, 0), (0, FACTS - 3)))
    outgoing = place_routes(route_ids.reshape(1, -1), hidden.reshape(-1, width_f), facts, experts)
    arrived = lax.all_to_all(
        outgoing.reshape(groups, local * CAP, -1), "expert", 0, 0, tiled=True
    )

    order = device_at(
        side[:, None, None], side[None, None, :], cores[None, :, None]
    ).reshape(-1)
    (rows,) = expert_rows(order, arrived, probe_signs, 1)
    lines = [
        [device_at(i, j, c) for i in range(SIDE) for c in range(CORES)] for j in range(SIDE)
    ]
    tangent_rows = lax.all_to_all(
        rows.reshape(SIDE * CORES, SIDE, local * CAP, -1),
        "expert",
        0,
        0,
        axis_index_groups=lines,
        tiled=True,
    )
    order = device_at(
        (x + side)[None, None, :] % SIDE,
        (y + side)[:, None, None] % SIDE,
        (core ^ cores)[None, :, None],
    ).reshape(-1)
    rows = expert_rows(order, arrived, down_weight, SIDE * CORES)
    primal_rows = [rows[0]]
    primal_rows += [
        shift(rows[i], 0, i // CORES, i % CORES) for i in range(1, SIDE * CORES)
    ]
    tangent_rows, *primal_rows = lax.optimization_barrier((tangent_rows, *primal_rows))
    arrived_all = lax.all_gather(arrived, "dp", axis=0, tiled=False)
    hidden_all = turned(arrived_all, local)

    (sums,) = middle_sums([tangent_rows], tokens)
    columns = [[device_at(i, j, c) for j in range(SIDE)] for i in range(SIDE) for c in range(CORES)]
    tangent = lax.all_to_all(sums, "expert", 0, 0, axis_index_groups=columns, tiled=True)
    sums = middle_sums(primal_rows, tokens)
    primal = [sums[0]] + [shift(sums[i], i, 0, 0) for i in range(1, SIDE)]

    part_row = part.astype(jnp.int32).reshape(1)
    grads = token_gradients(part_row, primal, tangent, layer_input, upstream, parts)
    grads = [grads[0]] + [
        lax.ppermute(grads[i], "dp", [(j, (j + i) % parts) for j in range(parts)])
        for i in range(1, parts)
    ]
    grads_all = lax.all_gather(jnp.stack(grads), "expert", axis=0, tiled=False)

    return estimate(part_row, arrived_all, hidden_all, grads_all, probe_signs)


def solution(mesh):
    in_specs = (
        P(("dp", "expert"), None),
        P(("dp", "expert"), None),
        P(("dp", "expert"), None, None),
        P(("dp", "expert"), None),
        P(("dp", "expert"), None),
        P("expert", None, None),
        P("expert", None, None),
    )
    out_specs = P("expert", None, "dp")
    return jax.shard_map(shards, mesh=mesh, in_specs=in_specs, out_specs=out_specs, check_vma=False)
```

time: 574 us -> 333 us (0.58)
  waiting for transfers between devices: 294 us -> 158 us
  blocking collectives: 128 us -> 44.1 us
  Pallas kernels: 0 us -> 81.2 us
  other arithmetic: 48.3 us -> 3.44 us
  local copies, waits for them, and re-layouts: 41.6 us -> 5.23 us
  matrix products: 30 us -> 0 us
  starting transfers between devices: 17.4 us -> 27.1 us
    reduce_scatter x1 -> x0, waiting for transfers between devices: 164 us -> none  [shards(): lax.psum_scatter(probe_signs.astype(jnp.float32) * curvature, 'dp', scatt...]
    all_to_all x2, waiting for transfers between devices: 130 us -> 0.01 us  [the longest x1 0.01 us: shards(): lax.all_to_all(rows.reshape(SIDE * CORES, SIDE, local * CAP, -1), 'expert...]
    ppermute x0 -> x13, waiting for transfers between devices: none -> 95.8 us  [the longest x10 90.5 us: shift(): return lax.ppermute(value, 'expert', pairs)]
    all_to_all x2 -> x1, blocking collectives: 128 us -> 44.1 us  [shards(): lax.all_to_all(outgoing.reshape(groups, local * CAP, -1), 'expert', 0, 0,...]
    pallas_call x0 -> x8, Pallas kernels: none -> 81.2 us  [the longest x2 23.4 us: expert_rows(): pl.pallas_call(rows_kernel, grid_spec=pltpu.PrefetchScalarGridSpec(num_sc...]
    all_gather x0 -> x2, waiting for transfers between devices: none -> 61.7 us  [the longest x1 61.6 us: shards(): grads_all = lax.all_gather(jnp.stack(grads), 'expert', axis=0, tiled=False)]
    dot_general x3 -> x0, matrix products: 30 us -> none  [the longest x1 11.6 us: shards(): jnp.einsum('slcf,slcd->lfd', arrived, arrived_grads, preferred_element_ty...]
    another operation x3 -> x2, other arithmetic: 27.2 us -> 1.78 us  [the longest x1 1.76 us: shards(): grads_all = lax.all_gather(jnp.stack(grads), 'expert', axis=0, tiled=False)]
  transfers between devices with their start and end apart: 3 -> 17, of which waited for: 3 -> 10; matrix products, arithmetic and copies ran while one was open for 4% -> 1% of each run, Pallas kernels for 0% -> 17%
where the time goes in v2:
time: 333 us; the launch traced here: 332 us
  waiting for transfers between devices  158 us (47%)
  Pallas kernels  81.2 us (24%)
  blocking collectives  44.1 us (13%)
  starting transfers between devices  27.1 us (8%)
  between operations  13.5 us (4%)
  local copies, waits for them, and re-layouts  5.23 us (2%)
  other arithmetic  3.44 us (1%)
    ppermute x10, waiting for transfers between devices, shift(): return lax.ppermute(value, 'expert', pairs)  90.5 us
    all_gather x1, waiting for transfers between devices, shards(): grads_all = lax.all_gather(jnp.stack(grads), 'expert', axis=0, tiled=False)  61.6 us
    all_to_all x1, blocking collectives, shards(): lax.all_to_all(outgoing.reshape(groups, local * CAP, -1), 'expert', 0, 0,...  44.1 us
    pallas_call x2, Pallas kernels, expert_rows(): pl.pallas_call(rows_kernel, grid_spec=pltpu.PrefetchScalarGridSpec(num_sc...  23.4 us
    pallas_call x1, Pallas kernels, estimate(): pl.pallas_call(estimate_kernel, grid_spec=pltpu.PrefetchScalarGridSpec(nu...  18.1 us
    pallas_call x2, Pallas kernels, middle_sums(): pl.pallas_call(middle_kernel, grid=(width // tile,), in_specs=row_specs +...  13.3 us
    pallas_call x1, Pallas kernels, turned(): pl.pallas_call(turn_kernel, grid=(parts, local), in_specs=[pl.BlockSpec((...  13 us
    ppermute x10, starting transfers between devices, shift(): return lax.ppermute(value, 'expert', pairs)  12.4 us
  transfers between devices with their start and end apart: 17, of which 10 were waited for; matrix products, arithmetic and copies ran while one was open for 1% of the time, Pallas kernels for 17%

profile of v2, /device:TPU:1, one launch (start us, length us, event | category | flops | bytes accessed | tf_op | source)
XLA Modules:
  0.0 332.2 jit_solution(14757742933840587531)
XLA Ops:
  8.2 0.8 copy.14
  9.9 0.8 pad.4.facts_ref
  10.6 6.8 %shard_map.73 = bf16[1536,896]{1,0:T(8,128)(2,1)} custom-call(s32[1,1024]{1,0:T(1,128)} %reshape.203.ids_ref, bf16[1024,768]{1,0:T(8,128)(2,1)} %bitcast.15, bf16[1024,128]{1,0:T(8,128)(2,1)} %pad.4.facts_ref), custom_call_target="tpu_custom_call" | custom-call | tf_op jit(solution)/shard_map/pallas_call | solution.py:60
  17.4 44.1 %all_to_all.15.x_ref = bf16[32,48,896]{2,1,0:T(8,128)(2,1)} all-to-all(bf16[32,48,896]{2,1,0:T(8,128)(2,1)} %bitcast.14), channel_id=1, replica_groups=mesh['dp'=4,'expert'=32] {'expert'}, dimensions={0} | all-to-all | bytes 5505024 | tf_op jit(solution)/shard_map/all_to_all | solution.py:341
  62.2 12.0 %shard_map.75 = bf16[32,48,2176]{2,1,0:T(8,128)(2,1)} custom-call(s32[32]{0:T(128)} %add.137.order_ref, bf16[32,48,896]{2,1,0:T(8,128)(2,1)} %all_to_all.15.x_ref, bf16[3,768,2048]{2,1,0:T(8,128)(2,1)} %probe_ref.1), custom_call_target="tpu_custom_call" | custom-call | flops 4831838208 | bytes 18874368 | tf_op jit(solution)/shard_map/pallas_call | solution.py:91
  74.2 4.8 %all-to-all-start.1 = ((bf16[8,4,48,2176]{3,2,1,0:T(8,128)(2,1)}), bf16[8,4,48,2176]{3,2,1,0:T(8,128)(2,1)}, u32[]{:S(2)}, u32[]{:S(2)}) async-start(bf16[8,4,48,2176]{3,2,1,0:T(8,128)(2,1)} %bitcast.12), calls=%async_computation.1 | async-start | bytes 13369344 | tf_op jit(solution)/shard_map/all_to_all | solution.py:352
  80.0 11.4 %shard_map.76 = (bf16[4,48,2176]{2,1,0:T(8,128)(2,1)}, bf16[4,48,2176]{2,1,0:T(8,128)(2,1)}, bf16[4,48,2176]{2,1,0:T(8,128)(2,1)}, bf16[4,48,2176]{2,1,0:T(8,128...) custom-call(s32[32]{0:T(128)} %add.152.order_ref, ...), custom_call_target="tpu_custom_call" | custom-call | flops 4831838208 | bytes 18874368 | tf_op jit(solution)/shard_map/pallas_call | solution.py:91
  92.1 3.9 %collective-permute-start.3 = (bf16[4,48,2176]{2,1,0:T(8,128)(2,1)}, bf16[4,48,2176]{2,1,0:T(8,128)(2,1)}, u32[]{:S(2)}, u32[]{:S(2)}) collective-permute-start(bf16[4,48,2176]{2,1,0:T(8,128)(2,1)} %get-tuple-element.34), channel_id=1, source_target_pairs={{0,4},{1,5},{2,6},{3,7},{4,0},{5,1},{6,2},{7,3},{8,12},{9,13},{10,... | collective-permute-start | bytes 2506760 | tf_op jit(solution)/shard_map/ppermute | solution.py:35
  95.9 2.1 collective-permute-start.5
  98.0 14.7 %collective-permute-done.1.refs_2_.refs_10_ = bf16[4,48,2176]{2,1,0:T(8,128)(2,1)} collective-permute-done((bf16[4,48,2176]{2,1,0:T(8,128)(2,1)}, bf16[4,48,2176]{2,1,0:T(8,128)(2,1)}, u32[]{:S(2)}, u32[]{:S(2)}) %collective-permute-start.1) | collective-permute-done | bytes 835616 | tf_op jit(solution)/shard_map/ppermute | solution.py:35
  112.7 1.3 collective-permute-start.6
  114.0 53.0 %collective-permute-done.2.refs_3_.refs_11_ = bf16[4,48,2176]{2,1,0:T(8,128)(2,1)} collective-permute-done((bf16[4,48,2176]{2,1,0:T(8,128)(2,1)}, bf16[4,48,2176]{2,1,0:T(8,128)(2,1)}, u32[]{:S(2)}, u32[]{:S(2)}) %collective-permute-start.2) | collective-permute-done | bytes 835616 | tf_op jit(solution)/shard_map/ppermute | solution.py:35
  167.0 1.0 collective-permute-done.6.refs_7_.refs_15_
  168.0 6.7 %shard_map.78 = bf16[4,128,2048]{2,1,0:T(8,128)(2,1)} custom-call(bf16[8,4,48,2176]{3,2,1,0:T(8,128)(2,1)} %all-to-all-done.1.refs_0_.refs_1_, bf16[8,4,48,2176]{3,2,1,0:T(8,128)(2,1)} %all-to-all-done.1.refs_0_.refs_1_), custom_call_target="tpu_custom_call" | custom-call | flops 1610612736 | bytes 6291456 | tf_op jit(solution)/shard_map/pallas_call | solution.py:173
  174.7 3.9 %all-to-all-start.2 = ((bf16[4,128,2048]{2,1,0:T(8,128)(2,1)}), bf16[4,128,2048]{2,1,0:T(8,128)(2,1)S(1)}, u32[]{:S(2)}, u32[]{:S(2)}) async-start(bf16[4,128,2048]{2,1,0:T(8,128)(2,1)} %shard_map.78), calls=%async_computation.2 | async-start | bytes 4194304 | tf_op jit(solution)/shard_map/all_to_all | solution.py:376
  178.6 6.6 %shard_map.77 = (f32[128,2048]{1,0:T(8,128)}, bf16[128,2048]{1,0:T(8,128)(2,1)}, bf16[128,2048]{1,0:T(8,128)(2,1)}, bf16[128,2048]{1,0:T(8,128)(2,1)}) custom-call(bf16[4,48,2176]{2,1,0:T(8,128)(2,1)} %get-tuple-element.38.refs_0_.refs_8_, bf16[4,48,2176]{2,1,0:T(8,128)(2,1)} %copy-done.1, bf16[4,48,2176]{2,1,0:T(8,128)(2,1)} %collective-permute-done.1.refs_2_.refs_10_, ...), custom_call_target="tpu_custom_call" | custom-call | flops 1610612736 | bytes 6291456 | tf_op jit(solution)/shard_map/pallas_call | solution.py:173
  185.2 0.9 collective-permute-start.7
  186.1 2.4 collective-permute-start.8
  188.5 1.2 collective-permute-start.9
  189.7 9.8 %collective-permute-done.7.refs_1_ = bf16[128,2048]{1,0:T(8,128)(2,1)S(1)} collective-permute-done((bf16[128,2048]{1,0:T(8,128)(2,1)}, bf16[128,2048]{1,0:T(8,128)(2,1)S(1)}, u32[]{:S(2)}, u32[]{:S(2)}) %collective-permute-start.7) | collective-permute-done | bytes 524320 | tf_op jit(solution)/shard_map/ppermute | solution.py:35
  199.5 11.8 %collective-permute-done.8.refs_2_ = bf16[128,2048]{1,0:T(8,128)(2,1)S(1)} collective-permute-done((bf16[128,2048]{1,0:T(8,128)(2,1)}, bf16[128,2048]{1,0:T(8,128)(2,1)S(1)}, u32[]{:S(2)}, u32[]{:S(2)}) %collective-permute-start.8) | collective-permute-done | bytes 524320 | tf_op jit(solution)/shard_map/ppermute | solution.py:35
  212.0 0.7 copy-done
  212.7 6.6 %shard_map.79 = (bf16[128,512]{1,0:T(8,128)(2,1)}, bf16[128,512]{1,0:T(8,128)(2,1)}, bf16[128,512]{1,0:T(8,128)(2,1)}, bf16[128,512]{1,0:T(8,128)(2,1)}) custom-call(s32[1]{0:T(128)} %bitcast.part_ref, f32[128,2048]{1,0:T(8,128)} %get-tuple-element.46.refs_0_, bf16[128,2048]{1,0:T(8,128)(2,1)} %copy-done.2, bf16[128,2048]{1,0:T(8,128)(2,1)} %copy-done.3, ...), custom_call_target="tpu_custom_call" | custom-call | tf_op jit(solution)/shard_map/pallas_call | solution.py:221
  219.4 1.9 collective-permute-start.10
  221.2 3.8 %collective-permute-start.11 = (bf16[128,512]{1,0:T(8,128)(2,1)}, bf16[128,512]{1,0:T(8,128)(2,1)S(1)}, u32[]{:S(2)}, u32[]{:S(2)}) collective-permute-start(bf16[128,512]{1,0:T(8,128)(2,1)} %get-tuple-element.53), channel_id=1, source_target_pairs={{0,64},{32,96},{64,0},{96,32},{1,65},{33,97},{65,1},{97,33},{2,66}... | collective-permute-start | bytes 393224 | tf_op jit(solution)/shard_map/ppermute | solution.py:383
  225.4 1.0 collective-permute-done.10
  226.4 3.3 collective-permute-done.11
  229.8 1.0 collective-permute-done.12
  230.8 1.8 pad_maximum_fusion
  232.6 13.0 %shard_map.74.hidden_ref = bf16[4,3,768,512]{3,2,1,0:T(8,128)(2,1)} custom-call(bf16[4,32,48,896]{3,2,1,0:T(8,128)(2,1)} %bitcast.10), custom_call_target="tpu_custom_call" | custom-call | bytes 22020096 | tf_op jit(solution)/shard_map/pallas_call | solution.py:244
  245.6 61.6 %all-gather.7.cloned.1.call-done = bf16[128,128,512]{2,1,0:T(8,128)(2,1)} async-done(((bf16[4,128,512]{2,1,0:T(8,128)(2,1)}), bf16[128,128,512]{2,1,0:T(8,128)(2,1)}) %all-gather.7.cloned.1.call-update) | async-done | bytes 16777232 | tf_op jit(solution)/shard_map/all_gather | solution.py:386
  307.2 18.1 %shard_map.80 = f32[3,768,512]{2,1,0:T(8,128)} custom-call(s32[1]{0:T(128)} %bitcast.part_ref, bf16[4,32,48,896]{3,2,1,0:T(8,128)(2,1)} %bitcast.11, bf16[4,3,768,512]{3,2,1,0:T(8,128)(2,1)} %shard_map.74.hidden_ref, bf16[32,4,128,512]{3,2,1,0:T(8,128)(2,1)} %bitcast.13, bf16[3,768,2048]{2,1,0:T(8,128)(2,1)} %probe_ref.1), custom_call_target="tpu_custom_call" | custom-call | flops 4831838208 | bytes 33292288 | tf_op jit(solution)/shard_map/pallas_call | solution.py:299
  (42 shorter events, 5.9 us)
Async XLA Ops:
  6.5 226.0 %all-gather.5.cloned.1.call-start = ((), (), s32[]{:S(2)}) async-start(), calls=%async_computation.3 | async-start | bytes 13762560 | tf_op jit(solution)/shard_map/all_gather | solution.py:371
  74.2 93.8 %all-to-all-start.1 = ((bf16[8,4,48,2176]{3,2,1,0:T(8,128)(2,1)}), bf16[8,4,48,2176]{3,2,1,0:T(8,128)(2,1)}, u32[]{:S(2)}, u32[]{:S(2)}) async-start(bf16[8,4,48,2176]{3,2,1,0:T(8,128)(2,1)} %bitcast.12), calls=%async_computation.1 | async-start | bytes 13369344 | tf_op jit(solution)/shard_map/all_to_all | solution.py:352
  91.4 4.6 %collective-permute-start = (bf16[4,48,2176]{2,1,0:T(8,128)(2,1)}, bf16[4,48,2176]{2,1,0:T(8,128)(2,1)S(1)}, u32[]{:S(2)}, u32[]{:S(2)}) collective-permute-start(bf16[4,48,2176]{2,1,0:T(8,128)(2,1)} %get-tuple-element.31), channel_id=1, source_target_pairs={{0,1},{1,0},{2,3},{3,2},{4,5},{5,4},{6,7},{7,6},{8,9},{9,8},{10,11... | collective-permute-start | bytes 2506760 | tf_op jit(solution)/shard_map/ppermute | solution.py:35
  91.4 21.3 %collective-permute-start.1 = (bf16[4,48,2176]{2,1,0:T(8,128)(2,1)}, bf16[4,48,2176]{2,1,0:T(8,128)(2,1)}, u32[]{:S(2)}, u32[]{:S(2)}) collective-permute-start(bf16[4,48,2176]{2,1,0:T(8,128)(2,1)} %get-tuple-element.32), channel_id=1, source_target_pairs={{0,2},{1,3},{2,4},{3,5},{4,6},{5,7},{6,0},{7,1},{8,10},{9,11},{10,... | collective-permute-start | bytes 2506760 | tf_op jit(solution)/shard_map/ppermute | solution.py:35
  91.5 75.6 %collective-permute-start.2 = (bf16[4,48,2176]{2,1,0:T(8,128)(2,1)}, bf16[4,48,2176]{2,1,0:T(8,128)(2,1)}, u32[]{:S(2)}, u32[]{:S(2)}) collective-permute-start(bf16[4,48,2176]{2,1,0:T(8,128)(2,1)} %get-tuple-element.33), channel_id=1, source_target_pairs={{0,3},{1,2},{2,5},{3,4},{4,7},{5,6},{6,1},{7,0},{8,11},{9,10},{10,... | collective-permute-start | bytes 2506760 | tf_op jit(solution)/shard_map/ppermute | solution.py:35
  92.1 75.0 %collective-permute-start.3 = (bf16[4,48,2176]{2,1,0:T(8,128)(2,1)}, bf16[4,48,2176]{2,1,0:T(8,128)(2,1)}, u32[]{:S(2)}, u32[]{:S(2)}) collective-permute-start(bf16[4,48,2176]{2,1,0:T(8,128)(2,1)} %get-tuple-element.34), channel_id=1, source_target_pairs={{0,4},{1,5},{2,6},{3,7},{4,0},{5,1},{6,2},{7,3},{8,12},{9,13},{10,... | collective-permute-start | bytes 2506760 | tf_op jit(solution)/shard_map/ppermute | solution.py:35
  95.9 71.1 %collective-permute-start.4 = (bf16[4,48,2176]{2,1,0:T(8,128)(2,1)}, bf16[4,48,2176]{2,1,0:T(8,128)(2,1)}, u32[]{:S(2)}, u32[]{:S(2)}) collective-permute-start(bf16[4,48,2176]{2,1,0:T(8,128)(2,1)} %get-tuple-element.35), channel_id=1, source_target_pairs={{0,5},{1,4},{2,7},{3,6},{4,1},{5,0},{6,3},{7,2},{8,13},{9,12},{10,... | collective-permute-start | bytes 2506760 | tf_op jit(solution)/shard_map/ppermute | solution.py:35
  95.9 78.8 %copy-start.1 = (bf16[4,48,2176]{2,1,0:T(8,128)(2,1)}, bf16[4,48,2176]{2,1,0:T(8,128)(2,1)S(1)}, u32[]{:S(2)}) copy-start(bf16[4,48,2176]{2,1,0:T(8,128)(2,1)S(1)} %collective-permute-done.refs_1_.refs_9_) | copy-start | bytes 2506756
  95.9 71.1 %collective-permute-start.5 = (bf16[4,48,2176]{2,1,0:T(8,128)(2,1)}, bf16[4,48,2176]{2,1,0:T(8,128)(2,1)}, u32[]{:S(2)}, u32[]{:S(2)}) collective-permute-start(bf16[4,48,2176]{2,1,0:T(8,128)(2,1)} %get-tuple-element.36), channel_id=1, source_target_pairs={{0,6},{1,7},{2,0},{3,1},{4,2},{5,3},{6,4},{7,5},{8,14},{9,15},{10,... | collective-permute-start | bytes 2506760 | tf_op jit(solution)/shard_map/ppermute | solution.py:35
  112.7 55.3 %collective-permute-start.6 = (bf16[4,48,2176]{2,1,0:T(8,128)(2,1)}, bf16[4,48,2176]{2,1,0:T(8,128)(2,1)}, u32[]{:S(2)}, u32[]{:S(2)}) collective-permute-start(bf16[4,48,2176]{2,1,0:T(8,128)(2,1)} %get-tuple-element.37), channel_id=1, source_target_pairs={{0,7},{1,6},{2,1},{3,0},{4,3},{5,2},{6,5},{7,4},{8,15},{9,14},{10,... | collective-permute-start | bytes 2506760 | tf_op jit(solution)/shard_map/ppermute | solution.py:35
  174.7 36.7 %all-to-all-start.2 = ((bf16[4,128,2048]{2,1,0:T(8,128)(2,1)}), bf16[4,128,2048]{2,1,0:T(8,128)(2,1)S(1)}, u32[]{:S(2)}, u32[]{:S(2)}) async-start(bf16[4,128,2048]{2,1,0:T(8,128)(2,1)} %shard_map.78), calls=%async_computation.2 | async-start | bytes 4194304 | tf_op jit(solution)/shard_map/all_to_all | solution.py:376
  178.6 128.7 %all-gather.7.cloned.1.call-start = ((), (), s32[]{:S(2)}) async-start(), calls=%async_computation.4 | async-start | bytes 17301504 | tf_op jit(solution)/shard_map/all_gather | solution.py:386
  185.2 14.3 %collective-permute-start.7 = (bf16[128,2048]{1,0:T(8,128)(2,1)}, bf16[128,2048]{1,0:T(8,128)(2,1)S(1)}, u32[]{:S(2)}, u32[]{:S(2)}) collective-permute-start(bf16[128,2048]{1,0:T(8,128)(2,1)} %get-tuple-element.47), channel_id=1, source_target_pairs={{0,8},{1,9},{2,10},{3,11},{4,12},{5,13},{6,14},{7,15},{8,16},{9,17... | collective-permute-start | bytes 1572872 | tf_op jit(solution)/shard_map/ppermute | solution.py:35
  186.1 25.2 %collective-permute-start.8 = (bf16[128,2048]{1,0:T(8,128)(2,1)}, bf16[128,2048]{1,0:T(8,128)(2,1)S(1)}, u32[]{:S(2)}, u32[]{:S(2)}) collective-permute-start(bf16[128,2048]{1,0:T(8,128)(2,1)} %get-tuple-element.48), channel_id=1, source_target_pairs={{0,16},{1,17},{2,18},{3,19},{4,20},{5,21},{6,22},{7,23},{8,24},{9,... | collective-permute-start | bytes 1572872 | tf_op jit(solution)/shard_map/ppermute | solution.py:35
  188.5 23.0 %collective-permute-start.9 = (bf16[128,2048]{1,0:T(8,128)(2,1)}, bf16[128,2048]{1,0:T(8,128)(2,1)}, u32[]{:S(2)}, u32[]{:S(2)}) collective-permute-start(bf16[128,2048]{1,0:T(8,128)(2,1)} %get-tuple-element.49), channel_id=1, source_target_pairs={{0,24},{1,25},{2,26},{3,27},{4,28},{5,29},{6,30},{7,31},{8,0},{9,1... | collective-permute-start | bytes 1572872 | tf_op jit(solution)/shard_map/ppermute | solution.py:35
  199.5 12.0 %copy-start.2 = (bf16[128,2048]{1,0:T(8,128)(2,1)}, bf16[128,2048]{1,0:T(8,128)(2,1)S(1)}, u32[]{:S(2)}) copy-start(bf16[128,2048]{1,0:T(8,128)(2,1)S(1)} %collective-permute-done.7.refs_1_) | copy-start | bytes 1572868
  211.2 0.8 copy-start.3
  211.4 1.3 copy-start
  219.4 7.1 %collective-permute-start.10 = (bf16[128,512]{1,0:T(8,128)(2,1)}, bf16[128,512]{1,0:T(8,128)(2,1)S(1)}, u32[]{:S(2)}, u32[]{:S(2)}) collective-permute-start(bf16[128,512]{1,0:T(8,128)(2,1)} %get-tuple-element.52), channel_id=1, source_target_pairs={{0,32},{32,64},{64,96},{96,0},{1,33},{33,65},{65,97},{97,1},{2,34}... | collective-permute-start | bytes 393224 | tf_op jit(solution)/shard_map/ppermute | solution.py:383
  221.2 8.5 %collective-permute-start.11 = (bf16[128,512]{1,0:T(8,128)(2,1)}, bf16[128,512]{1,0:T(8,128)(2,1)S(1)}, u32[]{:S(2)}, u32[]{:S(2)}) collective-permute-start(bf16[128,512]{1,0:T(8,128)(2,1)} %get-tuple-element.53), channel_id=1, source_target_pairs={{0,64},{32,96},{64,0},{96,32},{1,65},{33,97},{65,1},{97,33},{2,66}... | collective-permute-start | bytes 393224 | tf_op jit(solution)/shard_map/ppermute | solution.py:383
  225.1 5.7 %collective-permute-start.12 = (bf16[128,512]{1,0:T(8,128)(2,1)}, bf16[128,512]{1,0:T(8,128)(2,1)S(1)}, u32[]{:S(2)}, u32[]{:S(2)}) collective-permute-start(bf16[128,512]{1,0:T(8,128)(2,1)} %get-tuple-element.54), channel_id=1, source_target_pairs={{0,96},{32,0},{64,32},{96,64},{1,97},{33,1},{65,33},{97,65},{2,98}... | collective-permute-start | bytes 393224 | tf_op jit(solution)/shard_map/ppermute | solution.py:383
Sparse Core Ops, SparseCore 0:
  61.7 103.6 all-gather.4
  232.7 74.5 all-gather.6

commit v3 on v2

v3 whole, which is shorter than its diff:
```python
import jax
import jax.numpy as jnp
from jax import lax
from jax.experimental import pallas as pl
from jax.experimental.pallas import tpu as pltpu
from jax.sharding import PartitionSpec as P

EPSILON = 1e-06
CAP = 16
VMEM_LIMIT = 56 * 1024 * 1024
SIDE = 4
CORES = 2
F32 = jnp.float32
BF16 = jnp.bfloat16


def params():
    return pltpu.CompilerParams(vmem_limit_bytes=VMEM_LIMIT)


def dot(a, b, dims):
    return lax.dot_general(a, b, (dims, ((), ())), preferred_element_type=F32)


def device_at(x, y, core):
    return (x * SIDE + y) * CORES + core


def shift(value, dx, dy, core):
    pairs = []
    for i in range(SIDE * SIDE * CORES):
        x, y, c = i // (SIDE * CORES), i // CORES % SIDE, i % CORES
        pairs.append((i, device_at((x + dx) % SIDE, (y + dy) % SIDE, c ^ core)))
    return lax.ppermute(value, "expert", pairs)


def place_kernel(ids_ref, hidden_ref, out_ref, place_s):
    routes = hidden_ref.shape[0]
    experts = out_ref.shape[0] * pl.num_programs(0) // CAP
    step = out_ref.shape[0]

    @pl.when(pl.program_id(0) == 0)
    def _():
        ids = ids_ref[...]
        named = (lax.broadcasted_iota(jnp.int32, (experts, routes), 0) == ids).astype(F32)
        before = lax.broadcasted_iota(jnp.int32, (routes, routes), 0) < lax.broadcasted_iota(
            jnp.int32, (routes, routes), 1
        )
        earlier = dot(named.astype(BF16), before.astype(F32).astype(BF16), ((1,), (0,)))
        rank = jnp.sum(named * earlier, axis=0, keepdims=True)
        place_s[...] = ids * CAP + rank.astype(jnp.int32)

    slots = lax.broadcasted_iota(jnp.int32, (step, routes), 0) + pl.program_id(0) * step
    pick = (slots == place_s[...]).astype(F32).astype(BF16)
    out_ref[...] = dot(pick, hidden_ref[...], ((1,), (0,))).astype(BF16)


def place_routes(ids_row, hidden, experts):
    routes, width = hidden.shape
    step = 512
    return pl.pallas_call(
        place_kernel,
        grid=(experts * CAP // step,),
        in_specs=[
            pl.BlockSpec((1, routes), lambda i: (0, 0)),
            pl.BlockSpec((routes, width), lambda i: (0, 0)),
        ],
        out_specs=pl.BlockSpec((step, width), lambda i: (i, 0)),
        out_shape=jax.ShapeDtypeStruct((experts * CAP, width), BF16),
        scratch_shapes=[pltpu.VMEM((1, routes), jnp.int32)],
        compiler_params=params(),
    )(ids_row, hidden)


def rows_kernel(order_ref, x_ref, w_ref, *refs):
    *out_refs, x_s = refs
    groups, cap, width = x_ref.shape
    for j in range(groups):
        x_s[j * cap : (j + 1) * cap, :] = x_ref[order_ref[j]]
    width_d = w_ref.shape[2]
    each = groups // len(out_refs)
    tile = 1024
    for n in range(0, width_d, tile):
        rows = dot(x_s[...], w_ref[0, :, n : n + tile], ((1,), (0,))).astype(BF16)
        for j, out_ref in enumerate(out_refs):
            part = rows[j * each * cap : (j + 1) * each * cap]
            out_ref[:, :, n : n + tile] = part.reshape(each, cap, tile)


def expert_rows(order, arrived, weight, outs):
    groups, slots, _ = arrived.shape
    local, width_f, width_d = weight.shape
    each = groups // outs
    spec = pl.BlockSpec((each, CAP, width_d), lambda l, order: (0, l, 0))
    return pl.pallas_call(
        rows_kernel,
        grid_spec=pltpu.PrefetchScalarGridSpec(
            num_scalar_prefetch=1,
            grid=(local,),
            in_specs=[
                pl.BlockSpec((groups, CAP, width_f), lambda l, order: (0, l, 0)),
                pl.BlockSpec((1, width_f, width_d), lambda l, order: (l, 0, 0)),
            ],
            out_specs=[spec] * outs,
            scratch_shapes=[pltpu.VMEM((groups * CAP, width_f), BF16)],
        ),
        out_shape=[jax.ShapeDtypeStruct((each, slots, width_d), BF16)] * outs,
        cost_estimate=pl.CostEstimate(
            flops=2 * groups * slots * width_f * width_d,
            bytes_accessed=2 * (weight.size + arrived.size + groups * slots * width_d),
            transcendentals=0,
        ),
        compiler_params=params(),
    )(order, arrived, weight)


def selection(rank, weight):
    experts, tokens = rank.shape
    slot = lax.broadcasted_iota(jnp.int32, (CAP, tokens), 0)
    parts = [
        jnp.where(rank[e : e + 1, :] == slot, weight[e : e + 1, :], 0.0) for e in range(experts)
    ]
    return jnp.concatenate(parts, axis=0)


def split_high_low(x):
    high = x.astype(BF16)
    return high, (x - high.astype(F32)).astype(BF16)


def middle_kernel(rank_ref, weight_ref, tangent_ref, *refs):
    count = SIDE * CORES
    primal_refs, tangent_out = refs[:count], refs[count]
    primal_outs, sel_s = refs[count + 1 : -1], refs[-1]
    owners, tokens, _ = tangent_out.shape

    @pl.when(pl.program_id(0) == 0)
    def _():
        for i in range(2):
            for o in range(owners):
                high, low = split_high_low(selection(rank_ref[i, o], weight_ref[i, o]).T)
                sel_s[i, o, :tokens] = high
                sel_s[i, o, tokens:] = low

    for o in range(owners):
        rows = tangent_ref[:, o].reshape(-1, tangent_ref.shape[-1])
        both = dot(sel_s[0, o], rows, ((1,), (0,)))
        tangent_out[o] = (both[:tokens] + both[tokens:]).astype(BF16)
        rows = jnp.concatenate([ref[o] for ref in primal_refs], axis=0)
        both = dot(sel_s[1, o], rows, ((1,), (0,)))
        primal_outs[o][...] = (both[:tokens] + both[tokens:]).astype(primal_outs[o].dtype)


def middle_sums(rank, weight, tangent, primal):
    _, owners, experts, tokens = rank.shape
    sources = len(primal)
    slots, width = primal[0].shape[-2:]
    tile = 512
    whole = pl.BlockSpec(rank.shape, lambda n: (0, 0, 0, 0))
    return pl.pallas_call(
        middle_kernel,
        grid=(width // tile,),
        in_specs=[whole, whole]
        + [pl.BlockSpec((sources, owners, slots, tile), lambda n: (0, 0, 0, n))]
        + [pl.BlockSpec((owners, slots, tile), lambda n: (0, 0, n))] * sources,
        out_specs=[pl.BlockSpec((owners, tokens, tile), lambda n: (0, 0, n))]
        + [pl.BlockSpec((tokens, tile), lambda n: (0, n))] * owners,
        out_shape=[jax.ShapeDtypeStruct((owners, tokens, width), BF16)]
        + [jax.ShapeDtypeStruct((tokens, width), F32)]
        + [jax.ShapeDtypeStruct((tokens, width), BF16)] * (owners - 1),
        scratch_shapes=[pltpu.VMEM((2, owners, 2 * tokens, experts * CAP), BF16)],
        cost_estimate=pl.CostEstimate(
            flops=8 * owners * sources * slots * tokens * width,
            bytes_accessed=4 * owners * sources * slots * width,
            transcendentals=0,
        ),
        compiler_params=params(),
    )(rank, weight, tangent, *primal)


def token_kernel(part_ref, *refs):
    primal, tangent = refs[:SIDE], refs[SIDE]
    li_ref, up_ref = refs[SIDE + 1 : SIDE + 3]
    out_refs, grad_s = refs[SIDE + 3 : -1], refs[-1]
    summed = li_ref[...].astype(F32)
    for ref in primal:
        summed += ref[...].astype(F32)
    mt = tangent[0].astype(F32)
    for i in range(1, SIDE):
        mt += tangent[i].astype(F32)
    up = up_ref[...].astype(F32)
    width = up.shape[1]
    inverse = lax.rsqrt(jnp.sum(summed * summed, axis=1, keepdims=True) / width + EPSILON)
    cube = inverse * inverse * inverse
    a = jnp.sum(up * summed, axis=1, keepdims=True) / width
    s = jnp.sum(summed * mt, axis=1, keepdims=True) / width
    u = jnp.sum(up * mt, axis=1, keepdims=True) / width
    by_summed = 3.0 * cube * inverse * inverse * s * a - cube * u
    grad = (-cube * s) * up + by_summed * summed - (cube * a) * mt
    parts = len(out_refs)
    quarter = width // parts
    for p in range(parts):
        grad_s[p] = grad[:, p * quarter : (p + 1) * quarter].astype(BF16)
    for p in range(parts):
        out_refs[p][...] = grad_s[(part_ref[0] + p) % parts]


def token_gradients(part, primal, tangent, layer_input, upstream, parts):
    tokens, width = layer_input.shape
    tile = 32
    quarter = width // parts
    spec = pl.BlockSpec((tile, width), lambda n, part: (n, 0))
    return pl.pallas_call(
        token_kernel,
        grid_spec=pltpu.PrefetchScalarGridSpec(
            num_scalar_prefetch=1,
            grid=(tokens // tile,),
            in_specs=[spec] * SIDE
            + [pl.BlockSpec((SIDE, tile, width), lambda n, part: (0, n, 0)), spec, spec],
            out_specs=[pl.BlockSpec((tile, quarter), lambda n, part: (n, 0))] * parts,
            scratch_shapes=[pltpu.VMEM((parts, tile, quarter), BF16)],
        ),
        out_shape=[jax.ShapeDtypeStruct((tokens, quarter), BF16)] * parts,
        compiler_params=params(),
    )(part, *primal, tangent, layer_input, upstream)


def turn_kernel(hidden_ref, out_ref):
    _, groups, cap, width = hidden_ref.shape
    out_ref[0, 0] = hidden_ref[0].reshape(groups * cap, width).T


def turned(hidden, local):
    parts, groups, slots, width = hidden.shape
    return pl.pallas_call(
        turn_kernel,
        grid=(parts, local),
        in_specs=[pl.BlockSpec((1, groups, CAP, width), lambda g, l: (g, 0, l, 0))],
        out_specs=pl.BlockSpec((1, 1, width, groups * CAP), lambda g, l: (g, l, 0, 0)),
        out_shape=jax.ShapeDtypeStruct((parts, local, width, groups * CAP), BF16),
        cost_estimate=pl.CostEstimate(
            flops=0, bytes_accessed=4 * hidden.size, transcendentals=0
        ),
        compiler_params=params(),
    )(hidden)


def estimate_kernel(
    part_ref, rank_ref, weight_ref, hidden_ref, grad_ref, probe_ref, out_ref, rows_s, total_s
):
    step = pl.program_id(0)
    groups, _, tokens, quarter = grad_ref.shape
    local = total_s.shape[0]
    steps = pl.num_programs(0) - local
    slots = local * CAP
    nothing = jnp.zeros((slots, tokens), BF16)

    @pl.when(step < steps)
    def _():
        for i in range(0, groups, 2):
            high0, low0 = split_high_low(selection(rank_ref[0, i], weight_ref[0, i]))
            high1, low1 = split_high_low(selection(rank_ref[0, i + 1], weight_ref[0, i + 1]))
            first = jnp.concatenate([high0, nothing, low0, nothing], axis=0)
            second = jnp.concatenate([nothing, high1, nothing, low1], axis=0)
            sel = jnp.concatenate([first, second], axis=1)
            grads = grad_ref[i : i + 2, 0].reshape(2 * tokens, quarter)
            both = dot(sel, grads, ((1,), (0,)))
            rows = (both[: 2 * slots] + both[2 * slots :]).astype(BF16)
            for j in range(2):
                for l in range(local):
                    start = j * slots + l * CAP
                    rows_s[l, (i + j) * CAP : (i + j + 1) * CAP, :] = rows[start : start + CAP]

    for l in range(local):

        @pl.when(step == 0)
        def _():
            total_s[l] = dot(hidden_ref[0, l], rows_s[l], ((1,), (0,)))

        @pl.when(jnp.logical_and(step > 0, step < steps))
        def _():
            total_s[l] += dot(hidden_ref[0, l], rows_s[l], ((1,), (0,)))

    @pl.when(step >= steps)
    def _():
        out_ref[0] = total_s[step - steps] * probe_ref[0].astype(F32)


def estimate(part, rank, weight, hidden, grads, probe):
    parts, local, width_f, slots = hidden.shape
    groups, _, tokens, quarter = grads.shape

    def group(s, part):
        return (part[0] + parts - jnp.minimum(s, parts - 1)) % parts

    def expert(s):
        return jnp.maximum(s - parts, 0)

    routes = pl.BlockSpec((1, groups, local, tokens), lambda s, p: (group(s, p), 0, 0, 0))
    return pl.pallas_call(
        estimate_kernel,
        grid_spec=pltpu.PrefetchScalarGridSpec(
            num_scalar_prefetch=1,
            grid=(parts + local,),
            in_specs=[
                routes,
                routes,
                pl.BlockSpec((1, local, width_f, slots), lambda s, p: (group(s, p), 0, 0, 0)),
                pl.BlockSpec(
                    (groups, 1, tokens, quarter), lambda s, p: (0, jnp.minimum(s, parts - 1), 0, 0)
                ),
                pl.BlockSpec((1, width_f, quarter), lambda s, p: (expert(s), 0, p[0])),
            ],
            out_specs=pl.BlockSpec((1, width_f, quarter), lambda s, p: (expert(s), 0, 0)),
            scratch_shapes=[
                pltpu.VMEM((local, slots, quarter), BF16),
                pltpu.VMEM((local, width_f, quarter), F32),
            ],
        ),
        out_shape=jax.ShapeDtypeStruct((local, width_f, quarter), F32),
        cost_estimate=pl.CostEstimate(
            flops=2 * parts * slots * local * width_f * quarter,
            bytes_accessed=2 * (hidden.size + grads.size) + 6 * local * width_f * quarter,
            transcendentals=0,
        ),
        compiler_params=params(),
    )(part, rank, weight, hidden, grads, probe)


def routes_to(experts, ids, weights):
    tokens = ids.shape[-1]
    match = ids[:, None, :, :] == experts[..., :, None, None]
    named = jnp.any(match, axis=2)
    weight = jnp.sum(jnp.where(match, weights[:, None, :, :], 0.0), axis=2)
    before = jnp.triu(jnp.ones((tokens, tokens), F32), 1).astype(BF16)
    earlier = jnp.einsum("blt,tu->blu", named.astype(BF16), before, preferred_element_type=F32)
    return jnp.where(named, earlier.astype(jnp.int32), -1), weight


def shards(layer_input, upstream, hidden, route_ids, route_prob, down_weight, probe_signs):
    tokens, top = route_ids.shape
    local, width_f, width_d = down_weight.shape
    groups, parts = lax.axis_size("expert"), lax.axis_size("dp")
    experts = local * groups
    me, part = lax.axis_index("expert"), lax.axis_index("dp")
    x, y, core = me // (SIDE * CORES), me // CORES % SIDE, me % CORES
    side, cores = jnp.arange(SIDE, dtype=jnp.int32), jnp.arange(CORES, dtype=jnp.int32)

    combine = route_prob / jnp.sum(route_prob, axis=1, keepdims=True)
    facts = jnp.concatenate([route_ids.T.astype(F32), combine.T], axis=0)
    lines = [facts] + [shift(facts, 0, i, 0) for i in range(1, SIDE)]
    lines += [facts] + [shift(facts, i, 0, 0) for i in range(1, SIDE)]
    outgoing = place_routes(route_ids.reshape(1, -1), hidden.reshape(-1, width_f), experts)
    arrived = lax.all_to_all(
        outgoing.reshape(groups, local * CAP, -1), "expert", 0, 0, tiled=True
    )

    arrived, *lines[:-1] = lax.optimization_barrier((arrived, *lines[:-1]))

    order = device_at(
        side[:, None, None], side[None, None, :], cores[None, :, None]
    ).reshape(-1)
    (rows,) = expert_rows(order, arrived, probe_signs, 1)
    rows, lines[-1] = lax.optimization_barrier((rows, lines[-1]))
    along_x = [
        [device_at(i, j, c) for i in range(SIDE) for c in range(CORES)] for j in range(SIDE)
    ]
    tangent_rows = lax.all_to_all(
        rows.reshape(SIDE * CORES, SIDE, local * CAP, -1),
        "expert",
        0,
        0,
        axis_index_groups=along_x,
        tiled=True,
    )
    order = device_at(
        (x + side)[None, None, :] % SIDE,
        (y + side)[:, None, None] % SIDE,
        (core ^ cores)[None, :, None],
    ).reshape(-1)
    rows = expert_rows(order, arrived, down_weight, SIDE * CORES)
    primal_rows = [rows[0]]
    primal_rows += [
        shift(rows[i], 0, i // CORES, i % CORES) for i in range(1, SIDE * CORES)
    ]
    arrived_all = lax.all_gather(arrived, "dp", axis=0, tiled=False)
    hidden_all = turned(arrived_all, local)

    steps = jnp.concatenate([(y - side) % SIDE, SIDE + -side % SIDE])
    chosen = jnp.take(jnp.stack(lines), steps, axis=0)
    devices = jnp.stack(
        [
            device_at(side[:, None], y, cores[None, :]).reshape(-1),
            device_at(x, (y - side[:, None]) % SIDE, core ^ cores[None, :]).reshape(-1),
        ]
    )
    listed = (devices[:, :, None] * local + jnp.arange(local, dtype=jnp.int32)).reshape(2, -1)
    rank, weight = routes_to(
        jnp.repeat(listed, SIDE, axis=0), chosen[:, :top].astype(jnp.int32), chosen[:, top:]
    )
    rank, weight = (a.reshape(2, SIDE, -1, tokens) for a in (rank, weight))

    tangent_rows, *primal_rows = lax.optimization_barrier((tangent_rows, *primal_rows))
    sums, *primal = middle_sums(rank, weight, tangent_rows, primal_rows)
    along_y = [[device_at(i, j, c) for j in range(SIDE)] for i in range(SIDE) for c in range(CORES)]
    tangent = lax.all_to_all(sums, "expert", 0, 0, axis_index_groups=along_y, tiled=True)
    primal = [primal[0]] + [shift(primal[i], i, 0, 0) for i in range(1, SIDE)]
    tangent, hidden_all = lax.optimization_barrier((tangent, hidden_all))

    part_row = part.astype(jnp.int32).reshape(1)
    grads = token_gradients(part_row, primal, tangent, layer_input, upstream, parts)
    grads = [grads[0]] + [
        lax.ppermute(grads[i], "dp", [(j, (j + i) % parts) for j in range(parts)])
        for i in range(1, parts)
    ]
    ids, weights, grads = lax.optimization_barrier((route_ids.T, combine.T, jnp.stack(grads)))
    grads_all = lax.all_gather(grads, "expert", axis=0, tiled=False)
    ids = lax.all_gather(ids, ("dp", "expert"), axis=0, tiled=False)
    weights = lax.all_gather(weights, ("dp", "expert"), axis=0, tiled=False)
    own = me * local + jnp.arange(local, dtype=jnp.int32)
    rank, weight = routes_to(own, ids, weights)
    rank = rank.reshape(parts, groups, local, tokens)
    weight = weight.reshape(parts, groups, local, tokens)
    return estimate(part_row, rank, weight, hidden_all, grads_all, probe_signs)


def solution(mesh):
    in_specs = (
        P(("dp", "expert"), None),
        P(("dp", "expert"), None),
        P(("dp", "expert"), None, None),
        P(("dp", "expert"), None),
        P(("dp", "expert"), None),
        P("expert", None, None),
        P("expert", None, None),
    )
    out_specs = P("expert", None, "dp")
    return jax.shard_map(shards, mesh=mesh, in_specs=in_specs, out_specs=out_specs, check_vma=False)
```

time: 333 us -> 319 us (0.958)
  waiting for transfers between devices: 158 us -> 100 us
  blocking collectives: 44.1 us -> 71.7 us
  starting transfers between devices: 27.1 us -> 45 us
  Pallas kernels: 81.2 us -> 73.4 us
    all_gather x0 -> x2, blocking collectives: none -> 71.7 us  [the longest x1 37.7 us: shards(): ids = lax.all_gather(ids, ('dp', 'expert'), axis=0, tiled=False)]
    all_gather x1, waiting for transfers between devices: 61.6 us -> 0.01 us  [shards(): grads_all = lax.all_gather(grads, 'expert', axis=0, tiled=False)]
    all_to_all x1 -> x0, blocking collectives: 44.1 us -> none  [shards(): lax.all_to_all(outgoing.reshape(groups, local * CAP, -1), 'expert', 0, 0,...]
    all_to_all x1 -> x2, waiting for transfers between devices: 0.01 us -> 9.83 us  [the longest x1 8.12 us: shards(): lax.all_to_all(sums, 'expert', 0, 0, axis_index_groups=along_y, tiled=True)]
    all_to_all x1 -> x2, starting transfers between devices: 3.89 us -> 12.6 us  [the longest x1 8.72 us: shards(): lax.all_to_all(outgoing.reshape(groups, local * CAP, -1), 'expert', 0, 0,...]
    ppermute x10 -> x16, starting transfers between devices: 12.4 us -> 20.4 us  [shift(): return lax.ppermute(value, 'expert', pairs)]
    ppermute x10 -> x16, waiting for transfers between devices: 90.5 us -> 85.4 us  [shift(): return lax.ppermute(value, 'expert', pairs)]
    pallas_call x3 -> x2, Pallas kernels: 20.1 us -> 15.6 us  [the longest x1 9.86 us: middle_sums(): pl.pallas_call(middle_kernel, grid=(width // tile,), in_specs=[whole, who...]
  transfers between devices with their start and end apart: 17 -> 24, of which waited for: 10 -> 10; matrix products, arithmetic and copies ran while one was open for 1% -> 3% of each run, Pallas kernels for 17% -> 14%
where the time goes in v3:
time: 319 us; the launch traced here: 318 us
  waiting for transfers between devices  100 us (31%)
  Pallas kernels  73.4 us (23%)
  blocking collectives  71.7 us (22%)
  starting transfers between devices  45 us (14%)
  between operations  13.7 us (4%)
  local copies, waits for them, and re-layouts  6.88 us (2%)
  other arithmetic  6.08 us (2%)
    ppermute x16, waiting for transfers between devices, shift(): return lax.ppermute(value, 'expert', pairs)  85.4 us
    all_gather x1, blocking collectives, shards(): ids = lax.all_gather(ids, ('dp', 'expert'), axis=0, tiled=False)  37.7 us
    all_gather x1, blocking collectives, shards(): weights = lax.all_gather(weights, ('dp', 'expert'), axis=0, tiled=False)  33.9 us
    pallas_call x2, Pallas kernels, expert_rows(): pl.pallas_call(rows_kernel, grid_spec=pltpu.PrefetchScalarGridSpec(num_sc...  22.6 us
    ppermute x16, starting transfers between devices, shift(): return lax.ppermute(value, 'expert', pairs)  20.4 us
    pallas_call x1, Pallas kernels, estimate(): pl.pallas_call(estimate_kernel, grid_spec=pltpu.PrefetchScalarGridSpec(nu...  17.9 us
    pallas_call x1, Pallas kernels, turned(): pl.pallas_call(turn_kernel, grid=(parts, local), in_specs=[pl.BlockSpec((...  12.6 us
    pallas_call x1, Pallas kernels, middle_sums(): pl.pallas_call(middle_kernel, grid=(width // tile,), in_specs=[whole, who...  9.86 us
  transfers between devices with their start and end apart: 24, of which 10 were waited for; matrix products, arithmetic and copies ran while one was open for 3% of the time, Pallas kernels for 14%

profile of v3, /device:TPU:1, one launch (start us, length us, event | category | flops | bytes accessed | tf_op | source)
XLA Modules:
  0.0 318.1 jit_solution(3567015507862711733)
XLA Ops:
  8.0 5.8 %shard_map.73 = bf16[1536,768]{1,0:T(8,128)(2,1)} custom-call(s32[1,1024]{1,0:T(1,128)} %reshape.325.ids_ref, bf16[1024,768]{1,0:T(8,128)(2,1)} %bitcast.55), custom_call_target="tpu_custom_call" | custom-call | tf_op jit(solution)/shard_map/pallas_call | solution.py:61
  13.8 8.7 %all-to-all-start = ((bf16[32,48,768]{2,1,0:T(8,128)(2,1)}), bf16[32,48,768]{2,1,0:T(8,128)(2,1)S(1)}, u32[]{:S(2)}, u32[]{:S(2)}) async-start(bf16[32,48,768]{2,1,0:T(8,128)(2,1)} %bitcast.51), calls=%async_computation | async-start | bytes 4718592 | tf_op jit(solution)/shard_map/all_to_all | solution.py:354
  22.6 3.0 collective-permute-start.4
  25.9 2.4 collective-permute-start.2
  29.5 22.4 %collective-permute-done.4 = f32[16,128]{1,0:T(8,128)S(1)} collective-permute-done((f32[16,128]{1,0:T(8,128)S(1)}, f32[16,128]{1,0:T(8,128)S(1)}, u32[]{:S(2)}, u32[]{:S(2)}) %collective-permute-start.4) | collective-permute-done | bytes 8224 | tf_op jit(solution)/shard_map/ppermute | solution.py:34
  51.9 1.7 all-to-all-done.x_ref
  53.7 1.4 copy-done
  56.5 11.7 %shard_map.74 = bf16[32,48,2048]{2,1,0:T(8,128)(2,1)} custom-call(s32[32]{0:T(128)} %add.307.order_ref, bf16[32,48,768]{2,1,0:T(8,128)(2,1)} %copy-done, bf16[3,768,2048]{2,1,0:T(8,128)(2,1)} %probe_ref.1), custom_call_target="tpu_custom_call" | custom-call | flops 4831838208 | bytes 18087936 | tf_op jit(solution)/shard_map/pallas_call | solution.py:95
  68.3 6.1 %all-to-all-start.1 = ((bf16[8,4,48,2048]{3,2,1,0:T(8,128)(2,1)}), bf16[8,4,48,2048]{3,2,1,0:T(8,128)(2,1)}, u32[]{:S(2)}, u32[]{:S(2)}) async-start(bf16[8,4,48,2048]{3,2,1,0:T(8,128)(2,1)} %bitcast.48), calls=%async_computation.1 | async-start | bytes 12582912 | tf_op jit(solution)/shard_map/all_to_all | solution.py:368
  76.0 10.9 %shard_map.75 = (bf16[4,48,2048]{2,1,0:T(8,128)(2,1)}, bf16[4,48,2048]{2,1,0:T(8,128)(2,1)}, bf16[4,48,2048]{2,1,0:T(8,128)(2,1)}, bf16[4,48,2048]{2,1,0:T(8,128...) custom-call(s32[32]{0:T(128)} %add.338.order_ref, ...), custom_call_target="tpu_custom_call" | custom-call | flops 4831838208 | bytes 18087936 | tf_op jit(solution)/shard_map/pallas_call | solution.py:95
  87.6 3.9 %collective-permute-start.9 = (bf16[4,48,2048]{2,1,0:T(8,128)(2,1)}, bf16[4,48,2048]{2,1,0:T(8,128)(2,1)S(1)}, u32[]{:S(2)}, u32[]{:S(2)}) collective-permute-start(bf16[4,48,2048]{2,1,0:T(8,128)(2,1)} %get-tuple-element.60), channel_id=1, source_target_pairs={{0,4},{1,5},{2,6},{3,7},{4,0},{5,1},{6,2},{7,3},{8,12},{9,13},{10,... | collective-permute-start | bytes 2359304 | tf_op jit(solution)/shard_map/ppermute | solution.py:34
  92.1 2.1 collective-permute-start.11
  94.2 13.1 %collective-permute-done.7.refs_2_ = bf16[4,48,2048]{2,1,0:T(8,128)(2,1)S(1)} collective-permute-done((bf16[4,48,2048]{2,1,0:T(8,128)(2,1)}, bf16[4,48,2048]{2,1,0:T(8,128)(2,1)S(1)}, u32[]{:S(2)}, u32[]{:S(2)}) %collective-permute-start.7) | collective-permute-done | bytes 786464 | tf_op jit(solution)/shard_map/ppermute | solution.py:34
  107.3 1.1 collective-permute-start.12
  110.6 47.7 %collective-permute-done.8.refs_3_ = bf16[4,48,2048]{2,1,0:T(8,128)(2,1)S(1)} collective-permute-done((bf16[4,48,2048]{2,1,0:T(8,128)(2,1)}, bf16[4,48,2048]{2,1,0:T(8,128)(2,1)S(1)}, u32[]{:S(2)}, u32[]{:S(2)}) %collective-permute-start.8) | collective-permute-done | bytes 786464 | tf_op jit(solution)/shard_map/ppermute | solution.py:34
  158.3 1.3 collective-permute-done.12.refs_7_
  159.7 9.9 %shard_map.76 = (bf16[4,128,2048]{2,1,0:T(8,128)(2,1)}, f32[128,2048]{1,0:T(8,128)}, bf16[128,2048]{1,0:T(8,128)(2,1)}, bf16[128,2048]{1,0:T(8,128)(2,1)}, bf16[128,2048]{1,0:T(8,128)(2,1)}) custom-call(s32[2,4,24,128]{3,2,1,0:T(8,128)} %bitcast.63, f32[2,4,24,128]{3,2,1,0:T(8,128)} %bitcast.58, bf16[8,4,48,2048]{3,2,1,0:T(8,128)(2,1)} %all-to-all-done.1.tangent_ref, ...), custom_call_target="tpu_custom_call" | custom-call | flops 3221225472 | bytes 12582912 | tf_op jit(solution)/shard_map/pallas_call | solution.py:160
  169.5 3.9 %all-to-all-start.2 = ((bf16[4,128,2048]{2,1,0:T(8,128)(2,1)}), bf16[4,128,2048]{2,1,0:T(8,128)(2,1)S(1)}, u32[]{:S(2)}, u32[]{:S(2)}) async-start(bf16[4,128,2048]{2,1,0:T(8,128)(2,1)} %get-tuple-element.77), calls=%async_computation.2 | async-start | bytes 4194304 | tf_op jit(solution)/shard_map/all_to_all | solution.py:406
  173.4 1.4 collective-permute-start.13
  174.8 2.4 collective-permute-start.14
  177.2 1.2 collective-permute-start.15
  178.4 12.6 %shard_map.77.hidden_ref = bf16[4,3,768,512]{3,2,1,0:T(8,128)(2,1)} custom-call(bf16[4,32,48,768]{3,2,1,0:T(8,128)(2,1)} %bitcast.50), custom_call_target="tpu_custom_call" | custom-call | bytes 18874368 | tf_op jit(solution)/shard_map/pallas_call | solution.py:235
  191.0 8.1 %all-to-all-done.2.refs_4_ = bf16[4,128,2048]{2,1,0:T(8,128)(2,1)S(1)} async-done(((bf16[4,128,2048]{2,1,0:T(8,128)(2,1)}), bf16[4,128,2048]{2,1,0:T(8,128)(2,1)S(1)}, u32[]{:S(2)}, u32[]{:S(2)}) %all-to-all-start.2) | async-done | bytes 2097184 | tf_op jit(solution)/shard_map/all_to_all | solution.py:406
  200.8 4.7 %shard_map.78 = (bf16[128,512]{1,0:T(8,128)(2,1)}, bf16[128,512]{1,0:T(8,128)(2,1)}, bf16[128,512]{1,0:T(8,128)(2,1)}, bf16[128,512]{1,0:T(8,128)(2,1)}) custom-call(s32[1]{0:T(128)} %bitcast.part_ref, f32[128,2048]{1,0:T(8,128)} %get-tuple-element.73.refs_0_, bf16[128,2048]{1,0:T(8,128)(2,1)} %copy-done.6, bf16[128,2048]{1,0:T(8,128)(2,1)} %copy-done.7, ...), custom_call_target="tpu_custom_call" | custom-call | tf_op jit(solution)/shard_map/pallas_call | solution.py:213
  205.5 1.9 collective-permute-start.16
  207.4 3.4 %collective-permute-start.17 = (bf16[128,512]{1,0:T(8,128)(2,1)}, bf16[128,512]{1,0:T(8,128)(2,1)S(1)}, u32[]{:S(2)}, u32[]{:S(2)}) collective-permute-start(bf16[128,512]{1,0:T(8,128)(2,1)} %get-tuple-element.81), channel_id=1, source_target_pairs={{0,64},{32,96},{64,0},{96,32},{1,65},{33,97},{65,1},{97,33},{2,66}... | collective-permute-start | bytes 393224 | tf_op jit(solution)/shard_map/ppermute | solution.py:413
  212.2 3.3 %collective-permute-done.17 = bf16[128,512]{1,0:T(8,128)(2,1)S(1)} collective-permute-done((bf16[128,512]{1,0:T(8,128)(2,1)}, bf16[128,512]{1,0:T(8,128)(2,1)S(1)}, u32[]{:S(2)}, u32[]{:S(2)}) %collective-permute-start.17) | collective-permute-done | bytes 131104 | tf_op jit(solution)/shard_map/ppermute | solution.py:413
  216.5 1.8 pad_maximum_fusion
  218.3 37.7 %all-gather.1 = s32[1024,128]{1,0:T(8,128)S(1)} all-gather(s32[8,128]{1,0:T(8,128)S(1)} %bitcast.64), channel_id=3, replica_groups=mesh['dp'=4,'expert'=32] {'dp','expert'}, dimensions={0}, use_global_device_ids=true | all-gather | bytes 528384 | tf_op jit(solution)/shard_map/all_gather | solution.py:418
  257.9 33.9 %all-gather.2 = f32[1024,128]{1,0:T(8,128)S(1)} all-gather(f32[8,128]{1,0:T(8,128)S(1)} %divide_bitcast_fusion), channel_id=4, replica_groups=mesh['dp'=4,'expert'=32] {'dp','expert'}, dimensions={0}, use_global_device_ids=true | all-gather | bytes 528384 | tf_op jit(solution)/shard_map/all_gather | solution.py:419
  291.8 1.5 fusion
  293.3 17.9 %shard_map.79 = f32[3,768,512]{2,1,0:T(8,128)} custom-call(s32[1]{0:T(128)} %bitcast.part_ref, s32[4,32,3,128]{3,2,1,0:T(4,128)} %bitcast.57, f32[4,32,3,128]{3,2,1,0:T(4,128)} %bitcast.56, bf16[4,3,768,512]{3,2,1,0:T(8,128)(2,1)} %shard_map.77.hidden_ref, bf16[32,4,128,512]{3,2,1,0:T(8,128)(2,1)} %bitcast.49, bf16[3,768,2048]{2,1,0:T(8,128)(2,1)} %probe_ref.1), custom_call_target="tpu_custom_call" | custom-call | flops 4831838208 | bytes 33292288 | tf_op jit(solution)/shard_map/pallas_call | solution.py:300
  (100 shorter events, 15.4 us)
Async XLA Ops:
  13.8 8.8 %copy-start.9 = (f32[128,8]{0,1:T(8,128)S(1)}, f32[128,8]{0,1:T(8,128)}, u32[]{:S(2)}) copy-start(f32[128,8]{0,1:T(8,128)} %param.11) | copy-start | bytes 12292
  13.8 8.8 %copy-start.8 = (s32[128,8]{0,1:T(8,128)S(1)}, s32[128,8]{0,1:T(8,128)}, u32[]{:S(2)}) copy-start(s32[128,8]{0,1:T(8,128)} %param.10) | copy-start | bytes 12292
  13.8 39.9 %all-to-all-start = ((bf16[32,48,768]{2,1,0:T(8,128)(2,1)}), bf16[32,48,768]{2,1,0:T(8,128)(2,1)S(1)}, u32[]{:S(2)}, u32[]{:S(2)}) async-start(bf16[32,48,768]{2,1,0:T(8,128)(2,1)} %bitcast.51), calls=%async_computation | async-start | bytes 4718592 | tf_op jit(solution)/shard_map/all_to_all | solution.py:354
  22.5 155.9 %all-gather.7.cloned.1.call-start = ((), (), s32[]{:S(2)}) async-start(), calls=%async_computation.3 | async-start | bytes 11796480 | tf_op jit(solution)/shard_map/all_gather | solution.py:386
  22.6 29.3 %collective-permute-start.4 = (f32[16,128]{1,0:T(8,128)S(1)}, f32[16,128]{1,0:T(8,128)S(1)}, u32[]{:S(2)}, u32[]{:S(2)}) collective-permute-start(f32[16,128]{1,0:T(8,128)S(1)} %pad_maximum_fusion.1), channel_id=1, source_target_pairs={{0,16},{1,17},{2,18},{3,19},{4,20},{5,21},{6,22},{7,23},{8,24},{9,... | collective-permute-start | bytes 24584 | tf_op jit(solution)/shard_map/ppermute | solution.py:34
  25.6 26.3 %collective-permute-start.3 = (f32[16,128]{1,0:T(8,128)S(1)}, f32[16,128]{1,0:T(8,128)S(1)}, u32[]{:S(2)}, u32[]{:S(2)}) collective-permute-start(f32[16,128]{1,0:T(8,128)S(1)} %pad_maximum_fusion.1), channel_id=1, source_target_pairs={{0,8},{1,9},{2,10},{3,11},{4,12},{5,13},{6,14},{7,15},{8,16},{9,17... | collective-permute-start | bytes 24584 | tf_op jit(solution)/shard_map/ppermute | solution.py:34
  25.9 26.0 %collective-permute-start.2 = (f32[16,128]{1,0:T(8,128)S(1)}, f32[16,128]{1,0:T(8,128)S(1)}, u32[]{:S(2)}, u32[]{:S(2)}) collective-permute-start(f32[16,128]{1,0:T(8,128)S(1)} %pad_maximum_fusion.1), channel_id=1, source_target_pairs={{0,6},{1,7},{2,0},{3,1},{4,2},{5,3},{6,4},{7,5},{8,14},{9,15},{10,... | collective-permute-start | bytes 24584 | tf_op jit(solution)/shard_map/ppermute | solution.py:34
  28.4 23.6 %collective-permute-start.1 = (f32[16,128]{1,0:T(8,128)S(1)}, f32[16,128]{1,0:T(8,128)S(1)}, u32[]{:S(2)}, u32[]{:S(2)}) collective-permute-start(f32[16,128]{1,0:T(8,128)S(1)} %pad_maximum_fusion.1), channel_id=1, source_target_pairs={{0,4},{1,5},{2,6},{3,7},{4,0},{5,1},{6,2},{7,3},{8,12},{9,13},{10,... | collective-permute-start | bytes 24584 | tf_op jit(solution)/shard_map/ppermute | solution.py:34
  28.9 23.0 %collective-permute-start = (f32[16,128]{1,0:T(8,128)S(1)}, f32[16,128]{1,0:T(8,128)S(1)}, u32[]{:S(2)}, u32[]{:S(2)}) collective-permute-start(f32[16,128]{1,0:T(8,128)S(1)} %pad_maximum_fusion.1), channel_id=1, source_target_pairs={{0,2},{1,3},{2,4},{3,5},{4,6},{5,7},{6,0},{7,1},{8,10},{9,11},{10,... | collective-permute-start | bytes 24584 | tf_op jit(solution)/shard_map/ppermute | solution.py:34
  53.6 1.4 copy-start
  55.1 13.2 %collective-permute-start.5 = (f32[16,128]{1,0:T(8,128)S(1)}, f32[16,128]{1,0:T(8,128)S(1)}, u32[]{:S(2)}, u32[]{:S(2)}) collective-permute-start(f32[16,128]{1,0:T(8,128)S(1)} %pad_maximum_fusion.1), channel_id=1, source_target_pairs={{0,24},{1,25},{2,26},{3,27},{4,28},{5,29},{6,30},{7,31},{8,0},{9,1... | collective-permute-start | bytes 24584 | tf_op jit(solution)/shard_map/ppermute | solution.py:34
  68.3 91.3 %all-to-all-start.1 = ((bf16[8,4,48,2048]{3,2,1,0:T(8,128)(2,1)}), bf16[8,4,48,2048]{3,2,1,0:T(8,128)(2,1)}, u32[]{:S(2)}, u32[]{:S(2)}) async-start(bf16[8,4,48,2048]{3,2,1,0:T(8,128)(2,1)} %bitcast.48), calls=%async_computation.1 | async-start | bytes 12582912 | tf_op jit(solution)/shard_map/all_to_all | solution.py:368
  86.9 5.2 %collective-permute-start.6 = (bf16[4,48,2048]{2,1,0:T(8,128)(2,1)}, bf16[4,48,2048]{2,1,0:T(8,128)(2,1)S(1)}, u32[]{:S(2)}, u32[]{:S(2)}) collective-permute-start(bf16[4,48,2048]{2,1,0:T(8,128)(2,1)} %get-tuple-element.57), channel_id=1, source_target_pairs={{0,1},{1,0},{2,3},{3,2},{4,5},{5,4},{6,7},{7,6},{8,9},{9,8},{10,11... | collective-permute-start | bytes 2359304 | tf_op jit(solution)/shard_map/ppermute | solution.py:34
  87.0 20.3 %collective-permute-start.7 = (bf16[4,48,2048]{2,1,0:T(8,128)(2,1)}, bf16[4,48,2048]{2,1,0:T(8,128)(2,1)S(1)}, u32[]{:S(2)}, u32[]{:S(2)}) collective-permute-start(bf16[4,48,2048]{2,1,0:T(8,128)(2,1)} %get-tuple-element.58), channel_id=1, source_target_pairs={{0,2},{1,3},{2,4},{3,5},{4,6},{5,7},{6,0},{7,1},{8,10},{9,11},{10,... | collective-permute-start | bytes 2359304 | tf_op jit(solution)/shard_map/ppermute | solution.py:34
  87.2 71.1 %collective-permute-start.8 = (bf16[4,48,2048]{2,1,0:T(8,128)(2,1)}, bf16[4,48,2048]{2,1,0:T(8,128)(2,1)S(1)}, u32[]{:S(2)}, u32[]{:S(2)}) collective-permute-start(bf16[4,48,2048]{2,1,0:T(8,128)(2,1)} %get-tuple-element.59), channel_id=1, source_target_pairs={{0,3},{1,2},{2,5},{3,4},{4,7},{5,6},{6,1},{7,0},{8,11},{9,10},{10,... | collective-permute-start | bytes 2359304 | tf_op jit(solution)/shard_map/ppermute | solution.py:34
  87.6 70.7 %collective-permute-start.9 = (bf16[4,48,2048]{2,1,0:T(8,128)(2,1)}, bf16[4,48,2048]{2,1,0:T(8,128)(2,1)S(1)}, u32[]{:S(2)}, u32[]{:S(2)}) collective-permute-start(bf16[4,48,2048]{2,1,0:T(8,128)(2,1)} %get-tuple-element.60), channel_id=1, source_target_pairs={{0,4},{1,5},{2,6},{3,7},{4,0},{5,1},{6,2},{7,3},{8,12},{9,13},{10,... | collective-permute-start | bytes 2359304 | tf_op jit(solution)/shard_map/ppermute | solution.py:34
  91.4 66.9 %collective-permute-start.10 = (bf16[4,48,2048]{2,1,0:T(8,128)(2,1)}, bf16[4,48,2048]{2,1,0:T(8,128)(2,1)}, u32[]{:S(2)}, u32[]{:S(2)}) collective-permute-start(bf16[4,48,2048]{2,1,0:T(8,128)(2,1)} %get-tuple-element.61), channel_id=1, source_target_pairs={{0,5},{1,4},{2,7},{3,6},{4,1},{5,0},{6,3},{7,2},{8,13},{9,12},{10,... | collective-permute-start | bytes 2359304 | tf_op jit(solution)/shard_map/ppermute | solution.py:34
  92.1 67.5 %copy-start.2 = (bf16[4,48,2048]{2,1,0:T(8,128)(2,1)}, bf16[4,48,2048]{2,1,0:T(8,128)(2,1)S(1)}, u32[]{:S(2)}) copy-start(bf16[4,48,2048]{2,1,0:T(8,128)(2,1)S(1)} %collective-permute-done.6.refs_1_) | copy-start | bytes 2359300
  92.1 66.2 %collective-permute-start.11 = (bf16[4,48,2048]{2,1,0:T(8,128)(2,1)}, bf16[4,48,2048]{2,1,0:T(8,128)(2,1)}, u32[]{:S(2)}, u32[]{:S(2)}) collective-permute-start(bf16[4,48,2048]{2,1,0:T(8,128)(2,1)} %get-tuple-element.62), channel_id=1, source_target_pairs={{0,6},{1,7},{2,0},{3,1},{4,2},{5,3},{6,4},{7,5},{8,14},{9,15},{10,... | collective-permute-start | bytes 2359304 | tf_op jit(solution)/shard_map/ppermute | solution.py:34
  107.3 52.3 %copy-start.3 = (bf16[4,48,2048]{2,1,0:T(8,128)(2,1)}, bf16[4,48,2048]{2,1,0:T(8,128)(2,1)S(1)}, u32[]{:S(2)}) copy-start(bf16[4,48,2048]{2,1,0:T(8,128)(2,1)S(1)} %collective-permute-done.7.refs_2_) | copy-start | bytes 2359300
  107.3 52.3 %collective-permute-start.12 = (bf16[4,48,2048]{2,1,0:T(8,128)(2,1)}, bf16[4,48,2048]{2,1,0:T(8,128)(2,1)}, u32[]{:S(2)}, u32[]{:S(2)}) collective-permute-start(bf16[4,48,2048]{2,1,0:T(8,128)(2,1)} %get-tuple-element.63), channel_id=1, source_target_pairs={{0,7},{1,6},{2,1},{3,0},{4,3},{5,2},{6,5},{7,4},{8,15},{9,14},{10,... | collective-permute-start | bytes 2359304 | tf_op jit(solution)/shard_map/ppermute | solution.py:34
  158.3 1.3 copy-start.4
  158.3 1.3 copy-start.5
  169.5 29.6 %all-to-all-start.2 = ((bf16[4,128,2048]{2,1,0:T(8,128)(2,1)}), bf16[4,128,2048]{2,1,0:T(8,128)(2,1)S(1)}, u32[]{:S(2)}, u32[]{:S(2)}) async-start(bf16[4,128,2048]{2,1,0:T(8,128)(2,1)} %get-tuple-element.77), calls=%async_computation.2 | async-start | bytes 4194304 | tf_op jit(solution)/shard_map/all_to_all | solution.py:406
  173.4 120.0 %all-gather.9.cloned.1.call-start = ((), (), s32[]{:S(2)}) async-start(), calls=%async_computation.4 | async-start | bytes 17301504 | tf_op jit(solution)/shard_map/all_gather | solution.py:417
  173.4 25.7 %collective-permute-start.13 = (bf16[128,2048]{1,0:T(8,128)(2,1)}, bf16[128,2048]{1,0:T(8,128)(2,1)S(1)}, u32[]{:S(2)}, u32[]{:S(2)}) collective-permute-start(bf16[128,2048]{1,0:T(8,128)(2,1)} %get-tuple-element.74), channel_id=1, source_target_pairs={{0,8},{1,9},{2,10},{3,11},{4,12},{5,13},{6,14},{7,15},{8,16},{9,17... | collective-permute-start | bytes 1572872 | tf_op jit(solution)/shard_map/ppermute | solution.py:34
  174.8 25.2 %collective-permute-start.14 = (bf16[128,2048]{1,0:T(8,128)(2,1)}, bf16[128,2048]{1,0:T(8,128)(2,1)S(1)}, u32[]{:S(2)}, u32[]{:S(2)}) collective-permute-start(bf16[128,2048]{1,0:T(8,128)(2,1)} %get-tuple-element.75), channel_id=1, source_target_pairs={{0,16},{1,17},{2,18},{3,19},{4,20},{5,21},{6,22},{7,23},{8,24},{9,... | collective-permute-start | bytes 1572872 | tf_op jit(solution)/shard_map/ppermute | solution.py:34
  177.2 22.8 %collective-permute-start.15 = (bf16[128,2048]{1,0:T(8,128)(2,1)}, bf16[128,2048]{1,0:T(8,128)(2,1)}, u32[]{:S(2)}, u32[]{:S(2)}) collective-permute-start(bf16[128,2048]{1,0:T(8,128)(2,1)} %get-tuple-element.76), channel_id=1, source_target_pairs={{0,24},{1,25},{2,26},{3,27},{4,28},{5,29},{6,30},{7,31},{8,0},{9,1... | collective-permute-start | bytes 1572872 | tf_op jit(solution)/shard_map/ppermute | solution.py:34
  199.1 1.5 copy-start.6
  205.5 6.7 %collective-permute-start.16 = (bf16[128,512]{1,0:T(8,128)(2,1)}, bf16[128,512]{1,0:T(8,128)(2,1)S(1)}, u32[]{:S(2)}, u32[]{:S(2)}) collective-permute-start(bf16[128,512]{1,0:T(8,128)(2,1)} %get-tuple-element.80), channel_id=1, source_target_pairs={{0,32},{32,64},{64,96},{96,0},{1,33},{33,65},{65,97},{97,1},{2,34}... | collective-permute-start | bytes 393224 | tf_op jit(solution)/shard_map/ppermute | solution.py:413
  207.4 8.1 %collective-permute-start.17 = (bf16[128,512]{1,0:T(8,128)(2,1)}, bf16[128,512]{1,0:T(8,128)(2,1)S(1)}, u32[]{:S(2)}, u32[]{:S(2)}) collective-permute-start(bf16[128,512]{1,0:T(8,128)(2,1)} %get-tuple-element.81), channel_id=1, source_target_pairs={{0,64},{32,96},{64,0},{96,32},{1,65},{33,97},{65,1},{97,33},{2,66}... | collective-permute-start | bytes 393224 | tf_op jit(solution)/shard_map/ppermute | solution.py:413
  210.8 5.7 %collective-permute-start.18 = (bf16[128,512]{1,0:T(8,128)(2,1)}, bf16[128,512]{1,0:T(8,128)(2,1)S(1)}, u32[]{:S(2)}, u32[]{:S(2)}) collective-permute-start(bf16[128,512]{1,0:T(8,128)(2,1)} %get-tuple-element.82), channel_id=1, source_target_pairs={{0,96},{32,0},{64,32},{96,64},{1,97},{33,1},{65,33},{97,65},{2,98}... | collective-permute-start | bytes 393224 | tf_op jit(solution)/shard_map/ppermute | solution.py:413
  (2 other events, 2.2 us)
Sparse Core Ops, SparseCore 0:
  55.2 90.9 all-gather.6
  218.4 74.1 all-gather.8

commit v4 on v3

--- a/solution.py
+++ b/solution.py
@@ -255,6 +255,10 @@
     slots = local * CAP
     nothing = jnp.zeros((slots, tokens), BF16)
 
+    @pl.when(step == 0)
+    def _():
+        total_s[...] = jnp.zeros(total_s.shape, F32)
+
     @pl.when(step < steps)
     def _():
         for i in range(0, groups, 2):
@@ -271,14 +275,7 @@
                     start = j * slots + l * CAP
                     rows_s[l, (i + j) * CAP : (i + j + 1) * CAP, :] = rows[start : start + CAP]
 
-    for l in range(local):
-
-        @pl.when(step == 0)
-        def _():
-            total_s[l] = dot(hidden_ref[0, l], rows_s[l], ((1,), (0,)))
-
-        @pl.when(jnp.logical_and(step > 0, step < steps))
-        def _():
+        for l in range(local):
             total_s[l] += dot(hidden_ref[0, l], rows_s[l], ((1,), (0,)))
 
     @pl.when(step >= steps)
@@ -413,10 +410,13 @@
         lax.ppermute(grads[i], "dp", [(j, (j + i) % parts) for j in range(parts)])
         for i in range(1, parts)
     ]
-    ids, weights, grads = lax.optimization_barrier((route_ids.T, combine.T, jnp.stack(grads)))
+    high = lax.reduce_precision(combine, 8, 7)
+    routes = jnp.concatenate([route_ids.astype(F32), high, combine - high], axis=1).T.astype(BF16)
+    routes, grads = lax.optimization_barrier((routes, jnp.stack(grads)))
     grads_all = lax.all_gather(grads, "expert", axis=0, tiled=False)
-    ids = lax.all_gather(ids, ("dp", "expert"), axis=0, tiled=False)
-    weights = lax.all_gather(weights, ("dp", "expert"), axis=0, tiled=False)
+    routes = lax.all_gather(routes, ("dp", "expert"), axis=0, tiled=False)
+    ids = routes[:, :top].astype(jnp.int32)
+    weights = routes[:, top : 2 * top].astype(F32) + routes[:, 2 * top :].astype(F32)
     own = me * local + jnp.arange(local, dtype=jnp.int32)
     rank, weight = routes_to(own, ids, weights)
     rank = rank.reshape(parts, groups, local, tokens)

time: 319 us -> 317 us (level)
  blocking collectives: 71.7 us -> 37.8 us
  waiting for transfers between devices: 100 us -> 133 us
    all_gather x2 -> x1, blocking collectives: 71.7 us -> 37.8 us  [shards(): routes = lax.all_gather(routes, ('dp', 'expert'), axis=0, tiled=False)]
    all_gather x1, waiting for transfers between devices: 0.01 us -> 32.9 us  [shards(): grads_all = lax.all_gather(grads, 'expert', axis=0, tiled=False)]
  transfers between devices with their start and end apart: 24 -> 24, of which waited for: 10 -> 11; matrix products, arithmetic and copies ran while one was open for 3% -> 3% of each run, Pallas kernels for 14% -> 14%
where the time goes in v4:
time: 317 us; the launch traced here: 316 us
  waiting for transfers between devices  133 us (42%)
  Pallas kernels  72.4 us (23%)
  starting transfers between devices  45 us (14%)
  blocking collectives  37.8 us (12%)
  between operations  13.7 us (4%)
  local copies, waits for them, and re-layouts  6.88 us (2%)
  other arithmetic  6.21 us (2%)
    ppermute x16, waiting for transfers between devices, shift(): return lax.ppermute(value, 'expert', pairs)  85.4 us
    all_gather x1, blocking collectives, shards(): routes = lax.all_gather(routes, ('dp', 'expert'), axis=0, tiled=False)  37.8 us
    all_gather x1, waiting for transfers between devices, shards(): grads_all = lax.all_gather(grads, 'expert', axis=0, tiled=False)  32.9 us
    pallas_call x2, Pallas kernels, expert_rows(): pl.pallas_call(rows_kernel, grid_spec=pltpu.PrefetchScalarGridSpec(num_sc...  22.7 us
    ppermute x16, starting transfers between devices, shift(): return lax.ppermute(value, 'expert', pairs)  20.4 us
    pallas_call x1, Pallas kernels, estimate(): pl.pallas_call(estimate_kernel, grid_spec=pltpu.PrefetchScalarGridSpec(nu...  16.7 us
    pallas_call x1, Pallas kernels, turned(): pl.pallas_call(turn_kernel, grid=(parts, local), in_specs=[pl.BlockSpec((...  12.6 us
    pallas_call x1, Pallas kernels, middle_sums(): pl.pallas_call(middle_kernel, grid=(width // tile,), in_specs=[whole, who...  9.87 us
  transfers between devices with their start and end apart: 24, of which 11 were waited for; matrix products, arithmetic and copies ran while one was open for 3% of the time, Pallas kernels for 14%

profile of v4, /device:TPU:1, one launch (start us, length us, event | category | flops | bytes accessed | tf_op | source)
XLA Modules:
  0.0 316.2 jit_solution(11666199094901336133)
XLA Ops:
  8.0 5.8 %shard_map.73 = bf16[1536,768]{1,0:T(8,128)(2,1)} custom-call(s32[1,1024]{1,0:T(1,128)} %reshape.325.ids_ref, bf16[1024,768]{1,0:T(8,128)(2,1)} %bitcast.55), custom_call_target="tpu_custom_call" | custom-call | tf_op jit(solution)/shard_map/pallas_call | solution.py:61
  13.8 8.7 %all-to-all-start = ((bf16[32,48,768]{2,1,0:T(8,128)(2,1)}), bf16[32,48,768]{2,1,0:T(8,128)(2,1)S(1)}, u32[]{:S(2)}, u32[]{:S(2)}) async-start(bf16[32,48,768]{2,1,0:T(8,128)(2,1)} %bitcast.52), calls=%async_computation | async-start | bytes 4718592 | tf_op jit(solution)/shard_map/all_to_all | solution.py:351
  22.6 3.0 collective-permute-start.4
  25.9 2.4 collective-permute-start.2
  29.5 22.4 %collective-permute-done.4 = f32[16,128]{1,0:T(8,128)S(1)} collective-permute-done((f32[16,128]{1,0:T(8,128)S(1)}, f32[16,128]{1,0:T(8,128)S(1)}, u32[]{:S(2)}, u32[]{:S(2)}) %collective-permute-start.4) | collective-permute-done | bytes 8224 | tf_op jit(solution)/shard_map/ppermute | solution.py:34
  51.9 1.7 all-to-all-done.x_ref
  53.7 1.4 copy-done
  56.5 11.8 %shard_map.74 = bf16[32,48,2048]{2,1,0:T(8,128)(2,1)} custom-call(s32[32]{0:T(128)} %add.310.order_ref, bf16[32,48,768]{2,1,0:T(8,128)(2,1)} %copy-done, bf16[3,768,2048]{2,1,0:T(8,128)(2,1)} %probe_ref.1), custom_call_target="tpu_custom_call" | custom-call | flops 4831838208 | bytes 18087936 | tf_op jit(solution)/shard_map/pallas_call | solution.py:95
  68.3 6.1 %all-to-all-start.1 = ((bf16[8,4,48,2048]{3,2,1,0:T(8,128)(2,1)}), bf16[8,4,48,2048]{3,2,1,0:T(8,128)(2,1)}, u32[]{:S(2)}, u32[]{:S(2)}) async-start(bf16[8,4,48,2048]{3,2,1,0:T(8,128)(2,1)} %bitcast.49), calls=%async_computation.1 | async-start | bytes 12582912 | tf_op jit(solution)/shard_map/all_to_all | solution.py:365
  76.1 10.9 %shard_map.75 = (bf16[4,48,2048]{2,1,0:T(8,128)(2,1)}, bf16[4,48,2048]{2,1,0:T(8,128)(2,1)}, bf16[4,48,2048]{2,1,0:T(8,128)(2,1)}, bf16[4,48,2048]{2,1,0:T(8,128...) custom-call(s32[32]{0:T(128)} %add.341.order_ref, ...), custom_call_target="tpu_custom_call" | custom-call | flops 4831838208 | bytes 18087936 | tf_op jit(solution)/shard_map/pallas_call | solution.py:95
  87.6 3.9 %collective-permute-start.9 = (bf16[4,48,2048]{2,1,0:T(8,128)(2,1)}, bf16[4,48,2048]{2,1,0:T(8,128)(2,1)S(1)}, u32[]{:S(2)}, u32[]{:S(2)}) collective-permute-start(bf16[4,48,2048]{2,1,0:T(8,128)(2,1)} %get-tuple-element.59), channel_id=1, source_target_pairs={{0,4},{1,5},{2,6},{3,7},{4,0},{5,1},{6,2},{7,3},{8,12},{9,13},{10,... | collective-permute-start | bytes 2359304 | tf_op jit(solution)/shard_map/ppermute | solution.py:34
  92.2 2.1 collective-permute-start.11
  94.3 13.1 %collective-permute-done.7.refs_2_ = bf16[4,48,2048]{2,1,0:T(8,128)(2,1)S(1)} collective-permute-done((bf16[4,48,2048]{2,1,0:T(8,128)(2,1)}, bf16[4,48,2048]{2,1,0:T(8,128)(2,1)S(1)}, u32[]{:S(2)}, u32[]{:S(2)}) %collective-permute-start.7) | collective-permute-done | bytes 786464 | tf_op jit(solution)/shard_map/ppermute | solution.py:34
  107.5 1.1 collective-permute-start.12
  110.8 47.7 %collective-permute-done.8.refs_3_ = bf16[4,48,2048]{2,1,0:T(8,128)(2,1)S(1)} collective-permute-done((bf16[4,48,2048]{2,1,0:T(8,128)(2,1)}, bf16[4,48,2048]{2,1,0:T(8,128)(2,1)S(1)}, u32[]{:S(2)}, u32[]{:S(2)}) %collective-permute-start.8) | collective-permute-done | bytes 786464 | tf_op jit(solution)/shard_map/ppermute | solution.py:34
  158.5 1.3 collective-permute-done.12.refs_7_
  159.8 9.9 %shard_map.76 = (bf16[4,128,2048]{2,1,0:T(8,128)(2,1)}, f32[128,2048]{1,0:T(8,128)}, bf16[128,2048]{1,0:T(8,128)(2,1)}, bf16[128,2048]{1,0:T(8,128)(2,1)}, bf16[128,2048]{1,0:T(8,128)(2,1)}) custom-call(s32[2,4,24,128]{3,2,1,0:T(8,128)} %bitcast.63, f32[2,4,24,128]{3,2,1,0:T(8,128)} %bitcast.58, bf16[8,4,48,2048]{3,2,1,0:T(8,128)(2,1)} %all-to-all-done.1.tangent_ref, ...), custom_call_target="tpu_custom_call" | custom-call | flops 3221225472 | bytes 12582912 | tf_op jit(solution)/shard_map/pallas_call | solution.py:160
  169.6 3.9 %all-to-all-start.2 = ((bf16[4,128,2048]{2,1,0:T(8,128)(2,1)}), bf16[4,128,2048]{2,1,0:T(8,128)(2,1)S(1)}, u32[]{:S(2)}, u32[]{:S(2)}) async-start(bf16[4,128,2048]{2,1,0:T(8,128)(2,1)} %get-tuple-element.76), calls=%async_computation.2 | async-start | bytes 4194304 | tf_op jit(solution)/shard_map/all_to_all | solution.py:403
  173.5 1.4 collective-permute-start.13
  174.9 2.4 collective-permute-start.14
  177.4 1.1 collective-permute-start.15
  178.5 12.6 %shard_map.77.hidden_ref = bf16[4,3,768,512]{3,2,1,0:T(8,128)(2,1)} custom-call(bf16[4,32,48,768]{3,2,1,0:T(8,128)(2,1)} %bitcast.51), custom_call_target="tpu_custom_call" | custom-call | bytes 18874368 | tf_op jit(solution)/shard_map/pallas_call | solution.py:235
  191.1 8.1 %all-to-all-done.2.refs_4_ = bf16[4,128,2048]{2,1,0:T(8,128)(2,1)S(1)} async-done(((bf16[4,128,2048]{2,1,0:T(8,128)(2,1)}), bf16[4,128,2048]{2,1,0:T(8,128)(2,1)S(1)}, u32[]{:S(2)}, u32[]{:S(2)}) %all-to-all-start.2) | async-done | bytes 2097184 | tf_op jit(solution)/shard_map/all_to_all | solution.py:403
  201.0 4.7 %shard_map.78 = (bf16[128,512]{1,0:T(8,128)(2,1)}, bf16[128,512]{1,0:T(8,128)(2,1)}, bf16[128,512]{1,0:T(8,128)(2,1)}, bf16[128,512]{1,0:T(8,128)(2,1)}) custom-call(s32[1]{0:T(128)} %bitcast.part_ref, f32[128,2048]{1,0:T(8,128)} %get-tuple-element.72.refs_0_, bf16[128,2048]{1,0:T(8,128)(2,1)} %copy-done.6, bf16[128,2048]{1,0:T(8,128)(2,1)} %copy-done.7, ...), custom_call_target="tpu_custom_call" | custom-call | tf_op jit(solution)/shard_map/pallas_call | solution.py:213
  205.7 1.8 collective-permute-start.16
  207.5 3.5 %collective-permute-start.17 = (bf16[128,512]{1,0:T(8,128)(2,1)}, bf16[128,512]{1,0:T(8,128)(2,1)S(1)}, u32[]{:S(2)}, u32[]{:S(2)}) collective-permute-start(bf16[128,512]{1,0:T(8,128)(2,1)} %get-tuple-element.80), channel_id=1, source_target_pairs={{0,64},{32,96},{64,0},{96,32},{1,65},{33,97},{65,1},{97,33},{2,66}... | collective-permute-start | bytes 393224 | tf_op jit(solution)/shard_map/ppermute | solution.py:410
  212.3 3.3 %collective-permute-done.17 = bf16[128,512]{1,0:T(8,128)(2,1)S(1)} collective-permute-done((bf16[128,512]{1,0:T(8,128)(2,1)}, bf16[128,512]{1,0:T(8,128)(2,1)S(1)}, u32[]{:S(2)}, u32[]{:S(2)}) %collective-permute-start.17) | collective-permute-done | bytes 131104 | tf_op jit(solution)/shard_map/ppermute | solution.py:410
  216.7 1.8 pad_maximum_fusion
  218.5 37.8 %all-gather.1 = bf16[3072,128]{1,0:T(8,128)(2,1)S(1)} all-gather(bf16[24,128]{1,0:T(8,128)(2,1)S(1)} %maximum_bitcast_fusion), channel_id=3, replica_groups=mesh['dp'=4,'expert'=32] {'dp','expert'}, dimensions={0}, use_global_device_ids=true | all-gather | bytes 792576 | tf_op jit(solution)/shard_map/all_gather | solution.py:417
  258.2 1.5 fusion
  259.7 32.9 %all-gather.8.cloned.1.call-done = bf16[128,128,512]{2,1,0:T(8,128)(2,1)} async-done(((bf16[4,128,512]{2,1,0:T(8,128)(2,1)}), bf16[128,128,512]{2,1,0:T(8,128)(2,1)}) %all-gather.8.cloned.1.call-update) | async-done | bytes 16777232 | tf_op jit(solution)/shard_map/all_gather | solution.py:416
  292.6 16.7 %shard_map.79 = f32[3,768,512]{2,1,0:T(8,128)} custom-call(s32[1]{0:T(128)} %bitcast.part_ref, s32[4,32,3,128]{3,2,1,0:T(4,128)} %bitcast.57, f32[4,32,3,128]{3,2,1,0:T(4,128)} %bitcast.56, bf16[4,3,768,512]{3,2,1,0:T(8,128)(2,1)} %shard_map.77.hidden_ref, bf16[32,4,128,512]{3,2,1,0:T(8,128)(2,1)} %bitcast.50, bf16[3,768,2048]{2,1,0:T(8,128)(2,1)} %probe_ref.1), custom_call_target="tpu_custom_call" | custom-call | flops 4831838208 | bytes 33292288 | tf_op jit(solution)/shard_map/pallas_call | solution.py:297
  (102 shorter events, 15.5 us)
Async XLA Ops:
  13.8 8.8 %copy-start.8 = (f32[128,8]{0,1:T(8,128)S(1)}, f32[128,8]{0,1:T(8,128)}, u32[]{:S(2)}) copy-start(f32[128,8]{0,1:T(8,128)} %param.11) | copy-start | bytes 12292
  13.8 8.8 %copy-start.9 = (s32[128,8]{0,1:T(8,128)S(1)}, s32[128,8]{0,1:T(8,128)}, u32[]{:S(2)}) copy-start(s32[128,8]{0,1:T(8,128)} %param.10) | copy-start | bytes 12292
  13.8 39.9 %all-to-all-start = ((bf16[32,48,768]{2,1,0:T(8,128)(2,1)}), bf16[32,48,768]{2,1,0:T(8,128)(2,1)S(1)}, u32[]{:S(2)}, u32[]{:S(2)}) async-start(bf16[32,48,768]{2,1,0:T(8,128)(2,1)} %bitcast.52), calls=%async_computation | async-start | bytes 4718592 | tf_op jit(solution)/shard_map/all_to_all | solution.py:351
  22.5 156.0 %all-gather.6.cloned.1.call-start = ((), (), s32[]{:S(2)}) async-start(), calls=%async_computation.3 | async-start | bytes 11796480 | tf_op jit(solution)/shard_map/all_gather | solution.py:383
  22.6 29.3 %collective-permute-start.4 = (f32[16,128]{1,0:T(8,128)S(1)}, f32[16,128]{1,0:T(8,128)S(1)}, u32[]{:S(2)}, u32[]{:S(2)}) collective-permute-start(f32[16,128]{1,0:T(8,128)S(1)} %pad_maximum_fusion.1), channel_id=1, source_target_pairs={{0,16},{1,17},{2,18},{3,19},{4,20},{5,21},{6,22},{7,23},{8,24},{9,... | collective-permute-start | bytes 24584 | tf_op jit(solution)/shard_map/ppermute | solution.py:34
  25.6 26.3 %collective-permute-start.3 = (f32[16,128]{1,0:T(8,128)S(1)}, f32[16,128]{1,0:T(8,128)S(1)}, u32[]{:S(2)}, u32[]{:S(2)}) collective-permute-start(f32[16,128]{1,0:T(8,128)S(1)} %pad_maximum_fusion.1), channel_id=1, source_target_pairs={{0,8},{1,9},{2,10},{3,11},{4,12},{5,13},{6,14},{7,15},{8,16},{9,17... | collective-permute-start | bytes 24584 | tf_op jit(solution)/shard_map/ppermute | solution.py:34
  25.9 26.0 %collective-permute-start.2 = (f32[16,128]{1,0:T(8,128)S(1)}, f32[16,128]{1,0:T(8,128)S(1)}, u32[]{:S(2)}, u32[]{:S(2)}) collective-permute-start(f32[16,128]{1,0:T(8,128)S(1)} %pad_maximum_fusion.1), channel_id=1, source_target_pairs={{0,6},{1,7},{2,0},{3,1},{4,2},{5,3},{6,4},{7,5},{8,14},{9,15},{10,... | collective-permute-start | bytes 24584 | tf_op jit(solution)/shard_map/ppermute | solution.py:34
  28.4 23.6 %collective-permute-start.1 = (f32[16,128]{1,0:T(8,128)S(1)}, f32[16,128]{1,0:T(8,128)S(1)}, u32[]{:S(2)}, u32[]{:S(2)}) collective-permute-start(f32[16,128]{1,0:T(8,128)S(1)} %pad_maximum_fusion.1), channel_id=1, source_target_pairs={{0,4},{1,5},{2,6},{3,7},{4,0},{5,1},{6,2},{7,3},{8,12},{9,13},{10,... | collective-permute-start | bytes 24584 | tf_op jit(solution)/shard_map/ppermute | solution.py:34
  28.9 23.0 %collective-permute-start = (f32[16,128]{1,0:T(8,128)S(1)}, f32[16,128]{1,0:T(8,128)S(1)}, u32[]{:S(2)}, u32[]{:S(2)}) collective-permute-start(f32[16,128]{1,0:T(8,128)S(1)} %pad_maximum_fusion.1), channel_id=1, source_target_pairs={{0,2},{1,3},{2,4},{3,5},{4,6},{5,7},{6,0},{7,1},{8,10},{9,11},{10,... | collective-permute-start | bytes 24584 | tf_op jit(solution)/shard_map/ppermute | solution.py:34
  53.7 1.4 copy-start
  55.1 13.3 %collective-permute-start.5 = (f32[16,128]{1,0:T(8,128)S(1)}, f32[16,128]{1,0:T(8,128)S(1)}, u32[]{:S(2)}, u32[]{:S(2)}) collective-permute-start(f32[16,128]{1,0:T(8,128)S(1)} %pad_maximum_fusion.1), channel_id=1, source_target_pairs={{0,24},{1,25},{2,26},{3,27},{4,28},{5,29},{6,30},{7,31},{8,0},{9,1... | collective-permute-start | bytes 24584 | tf_op jit(solution)/shard_map/ppermute | solution.py:34
  68.3 91.4 %all-to-all-start.1 = ((bf16[8,4,48,2048]{3,2,1,0:T(8,128)(2,1)}), bf16[8,4,48,2048]{3,2,1,0:T(8,128)(2,1)}, u32[]{:S(2)}, u32[]{:S(2)}) async-start(bf16[8,4,48,2048]{3,2,1,0:T(8,128)(2,1)} %bitcast.49), calls=%async_computation.1 | async-start | bytes 12582912 | tf_op jit(solution)/shard_map/all_to_all | solution.py:365
  87.0 5.2 %collective-permute-start.6 = (bf16[4,48,2048]{2,1,0:T(8,128)(2,1)}, bf16[4,48,2048]{2,1,0:T(8,128)(2,1)S(1)}, u32[]{:S(2)}, u32[]{:S(2)}) collective-permute-start(bf16[4,48,2048]{2,1,0:T(8,128)(2,1)} %get-tuple-element.56), channel_id=1, source_target_pairs={{0,1},{1,0},{2,3},{3,2},{4,5},{5,4},{6,7},{7,6},{8,9},{9,8},{10,11... | collective-permute-start | bytes 2359304 | tf_op jit(solution)/shard_map/ppermute | solution.py:34
  87.2 20.3 %collective-permute-start.7 = (bf16[4,48,2048]{2,1,0:T(8,128)(2,1)}, bf16[4,48,2048]{2,1,0:T(8,128)(2,1)S(1)}, u32[]{:S(2)}, u32[]{:S(2)}) collective-permute-start(bf16[4,48,2048]{2,1,0:T(8,128)(2,1)} %get-tuple-element.57), channel_id=1, source_target_pairs={{0,2},{1,3},{2,4},{3,5},{4,6},{5,7},{6,0},{7,1},{8,10},{9,11},{10,... | collective-permute-start | bytes 2359304 | tf_op jit(solution)/shard_map/ppermute | solution.py:34
  87.3 71.1 %collective-permute-start.8 = (bf16[4,48,2048]{2,1,0:T(8,128)(2,1)}, bf16[4,48,2048]{2,1,0:T(8,128)(2,1)S(1)}, u32[]{:S(2)}, u32[]{:S(2)}) collective-permute-start(bf16[4,48,2048]{2,1,0:T(8,128)(2,1)} %get-tuple-element.58), channel_id=1, source_target_pairs={{0,3},{1,2},{2,5},{3,4},{4,7},{5,6},{6,1},{7,0},{8,11},{9,10},{10,... | collective-permute-start | bytes 2359304 | tf_op jit(solution)/shard_map/ppermute | solution.py:34
  87.6 70.8 %collective-permute-start.9 = (bf16[4,48,2048]{2,1,0:T(8,128)(2,1)}, bf16[4,48,2048]{2,1,0:T(8,128)(2,1)S(1)}, u32[]{:S(2)}, u32[]{:S(2)}) collective-permute-start(bf16[4,48,2048]{2,1,0:T(8,128)(2,1)} %get-tuple-element.59), channel_id=1, source_target_pairs={{0,4},{1,5},{2,6},{3,7},{4,0},{5,1},{6,2},{7,3},{8,12},{9,13},{10,... | collective-permute-start | bytes 2359304 | tf_op jit(solution)/shard_map/ppermute | solution.py:34
  91.6 66.9 %collective-permute-start.10 = (bf16[4,48,2048]{2,1,0:T(8,128)(2,1)}, bf16[4,48,2048]{2,1,0:T(8,128)(2,1)}, u32[]{:S(2)}, u32[]{:S(2)}) collective-permute-start(bf16[4,48,2048]{2,1,0:T(8,128)(2,1)} %get-tuple-element.60), channel_id=1, source_target_pairs={{0,5},{1,4},{2,7},{3,6},{4,1},{5,0},{6,3},{7,2},{8,13},{9,12},{10,... | collective-permute-start | bytes 2359304 | tf_op jit(solution)/shard_map/ppermute | solution.py:34
  92.2 67.5 %copy-start.2 = (bf16[4,48,2048]{2,1,0:T(8,128)(2,1)}, bf16[4,48,2048]{2,1,0:T(8,128)(2,1)S(1)}, u32[]{:S(2)}) copy-start(bf16[4,48,2048]{2,1,0:T(8,128)(2,1)S(1)} %collective-permute-done.6.refs_1_) | copy-start | bytes 2359300
  92.2 66.2 %collective-permute-start.11 = (bf16[4,48,2048]{2,1,0:T(8,128)(2,1)}, bf16[4,48,2048]{2,1,0:T(8,128)(2,1)}, u32[]{:S(2)}, u32[]{:S(2)}) collective-permute-start(bf16[4,48,2048]{2,1,0:T(8,128)(2,1)} %get-tuple-element.61), channel_id=1, source_target_pairs={{0,6},{1,7},{2,0},{3,1},{4,2},{5,3},{6,4},{7,5},{8,14},{9,15},{10,... | collective-permute-start | bytes 2359304 | tf_op jit(solution)/shard_map/ppermute | solution.py:34
  107.5 52.3 %copy-start.3 = (bf16[4,48,2048]{2,1,0:T(8,128)(2,1)}, bf16[4,48,2048]{2,1,0:T(8,128)(2,1)S(1)}, u32[]{:S(2)}) copy-start(bf16[4,48,2048]{2,1,0:T(8,128)(2,1)S(1)} %collective-permute-done.7.refs_2_) | copy-start | bytes 2359300
  107.5 52.3 %collective-permute-start.12 = (bf16[4,48,2048]{2,1,0:T(8,128)(2,1)}, bf16[4,48,2048]{2,1,0:T(8,128)(2,1)}, u32[]{:S(2)}, u32[]{:S(2)}) collective-permute-start(bf16[4,48,2048]{2,1,0:T(8,128)(2,1)} %get-tuple-element.62), channel_id=1, source_target_pairs={{0,7},{1,6},{2,1},{3,0},{4,3},{5,2},{6,5},{7,4},{8,15},{9,14},{10,... | collective-permute-start | bytes 2359304 | tf_op jit(solution)/shard_map/ppermute | solution.py:34
  158.4 1.3 copy-start.4
  158.4 1.3 copy-start.5
  169.6 29.6 %all-to-all-start.2 = ((bf16[4,128,2048]{2,1,0:T(8,128)(2,1)}), bf16[4,128,2048]{2,1,0:T(8,128)(2,1)S(1)}, u32[]{:S(2)}, u32[]{:S(2)}) async-start(bf16[4,128,2048]{2,1,0:T(8,128)(2,1)} %get-tuple-element.76), calls=%async_computation.2 | async-start | bytes 4194304 | tf_op jit(solution)/shard_map/all_to_all | solution.py:403
  173.5 119.2 %all-gather.8.cloned.1.call-start = ((), (), s32[]{:S(2)}) async-start(), calls=%async_computation.4 | async-start | bytes 17301504 | tf_op jit(solution)/shard_map/all_gather | solution.py:416
  173.5 25.7 %collective-permute-start.13 = (bf16[128,2048]{1,0:T(8,128)(2,1)}, bf16[128,2048]{1,0:T(8,128)(2,1)S(1)}, u32[]{:S(2)}, u32[]{:S(2)}) collective-permute-start(bf16[128,2048]{1,0:T(8,128)(2,1)} %get-tuple-element.73), channel_id=1, source_target_pairs={{0,8},{1,9},{2,10},{3,11},{4,12},{5,13},{6,14},{7,15},{8,16},{9,17... | collective-permute-start | bytes 1572872 | tf_op jit(solution)/shard_map/ppermute | solution.py:34
  174.9 25.2 %collective-permute-start.14 = (bf16[128,2048]{1,0:T(8,128)(2,1)}, bf16[128,2048]{1,0:T(8,128)(2,1)S(1)}, u32[]{:S(2)}, u32[]{:S(2)}) collective-permute-start(bf16[128,2048]{1,0:T(8,128)(2,1)} %get-tuple-element.74), channel_id=1, source_target_pairs={{0,16},{1,17},{2,18},{3,19},{4,20},{5,21},{6,22},{7,23},{8,24},{9,... | collective-permute-start | bytes 1572872 | tf_op jit(solution)/shard_map/ppermute | solution.py:34
  177.4 22.8 %collective-permute-start.15 = (bf16[128,2048]{1,0:T(8,128)(2,1)}, bf16[128,2048]{1,0:T(8,128)(2,1)}, u32[]{:S(2)}, u32[]{:S(2)}) collective-permute-start(bf16[128,2048]{1,0:T(8,128)(2,1)} %get-tuple-element.75), channel_id=1, source_target_pairs={{0,24},{1,25},{2,26},{3,27},{4,28},{5,29},{6,30},{7,31},{8,0},{9,1... | collective-permute-start | bytes 1572872 | tf_op jit(solution)/shard_map/ppermute | solution.py:34
  199.2 1.5 copy-start.6
  205.7 6.7 %collective-permute-start.16 = (bf16[128,512]{1,0:T(8,128)(2,1)}, bf16[128,512]{1,0:T(8,128)(2,1)S(1)}, u32[]{:S(2)}, u32[]{:S(2)}) collective-permute-start(bf16[128,512]{1,0:T(8,128)(2,1)} %get-tuple-element.79), channel_id=1, source_target_pairs={{0,32},{32,64},{64,96},{96,0},{1,33},{33,65},{65,97},{97,1},{2,34}... | collective-permute-start | bytes 393224 | tf_op jit(solution)/shard_map/ppermute | solution.py:410
  207.5 8.2 %collective-permute-start.17 = (bf16[128,512]{1,0:T(8,128)(2,1)}, bf16[128,512]{1,0:T(8,128)(2,1)S(1)}, u32[]{:S(2)}, u32[]{:S(2)}) collective-permute-start(bf16[128,512]{1,0:T(8,128)(2,1)} %get-tuple-element.80), channel_id=1, source_target_pairs={{0,64},{32,96},{64,0},{96,32},{1,65},{33,97},{65,1},{97,33},{2,66}... | collective-permute-start | bytes 393224 | tf_op jit(solution)/shard_map/ppermute | solution.py:410
  211.0 5.7 %collective-permute-start.18 = (bf16[128,512]{1,0:T(8,128)(2,1)}, bf16[128,512]{1,0:T(8,128)(2,1)S(1)}, u32[]{:S(2)}, u32[]{:S(2)}) collective-permute-start(bf16[128,512]{1,0:T(8,128)(2,1)} %get-tuple-element.81), channel_id=1, source_target_pairs={{0,96},{32,0},{64,32},{96,64},{1,97},{33,1},{65,33},{97,65},{2,98}... | collective-permute-start | bytes 393224 | tf_op jit(solution)/shard_map/ppermute | solution.py:410
  (2 other events, 2.1 us)
Sparse Core Ops, SparseCore 0:
  55.2 90.9 all-gather.5
  218.6 74.0 all-gather.7

commit v5 on v4

--- a/solution.py
+++ b/solution.py
@@ -7,9 +7,10 @@
 
 EPSILON = 1e-06
 CAP = 16
-VMEM_LIMIT = 56 * 1024 * 1024
+VMEM_LIMIT = 62 * 1024 * 1024
 SIDE = 4
 CORES = 2
+LANES = 128
 F32 = jnp.float32
 BF16 = jnp.bfloat16
 
@@ -43,10 +44,12 @@
     def _():
         ids = ids_ref[...]
         named = (lax.broadcasted_iota(jnp.int32, (experts, routes), 0) == ids).astype(F32)
-        before = lax.broadcasted_iota(jnp.int32, (routes, routes), 0) < lax.broadcasted_iota(
-            jnp.int32, (routes, routes), 1
-        )
-        earlier = dot(named.astype(BF16), before.astype(F32).astype(BF16), ((1,), (0,)))
+        token = lax.broadcasted_iota(jnp.int32, (LANES, routes), 0)
+        owner = lax.broadcasted_iota(jnp.int32, (LANES, routes), 1) // (routes // LANES)
+        own = (token == owner).astype(F32).astype(BF16)
+        after = (token < owner).astype(F32).astype(BF16)
+        by_token = dot(named.astype(BF16), own, ((1,), (1,))).astype(BF16)
+        earlier = dot(by_token, after, ((1,), (0,)))
         rank = jnp.sum(named * earlier, axis=0, keepdims=True)
         place_s[...] = ids * CAP + rank.astype(jnp.int32)
 

time: 317 us -> 318 us (level)
  no operation moved by 1% of the time
where the time goes in v5:
time: 318 us; the launch traced here: 317 us
  waiting for transfers between devices  133 us (42%)
  Pallas kernels  72.2 us (23%)
  starting transfers between devices  45.7 us (14%)
  blocking collectives  38 us (12%)
  between operations  13.7 us (4%)
  local copies, waits for them, and re-layouts  7.05 us (2%)
  other arithmetic  6.2 us (2%)
    ppermute x16, waiting for transfers between devices, shift(): return lax.ppermute(value, 'expert', pairs)  85.5 us
    all_gather x1, blocking collectives, shards(): routes = lax.all_gather(routes, ('dp', 'expert'), axis=0, tiled=False)  38 us
    all_gather x1, waiting for transfers between devices, shards(): grads_all = lax.all_gather(grads, 'expert', axis=0, tiled=False)  32.8 us
    pallas_call x2, Pallas kernels, expert_rows(): pl.pallas_call(rows_kernel, grid_spec=pltpu.PrefetchScalarGridSpec(num_sc...  22.6 us
    ppermute x16, starting transfers between devices, shift(): return lax.ppermute(value, 'expert', pairs)  20.5 us
    pallas_call x1, Pallas kernels, estimate(): pl.pallas_call(estimate_kernel, grid_spec=pltpu.PrefetchScalarGridSpec(nu...  16.7 us
    pallas_call x1, Pallas kernels, turned(): pl.pallas_call(turn_kernel, grid=(parts, local), in_specs=[pl.BlockSpec((...  12.6 us
    pallas_call x1, Pallas kernels, middle_sums(): pl.pallas_call(middle_kernel, grid=(width // tile,), in_specs=[whole, who...  9.86 us
  transfers between devices with their start and end apart: 24, of which 11 were waited for; matrix products, arithmetic and copies ran while one was open for 3% of the time, Pallas kernels for 14%

profile of v5, /device:TPU:1, one launch (start us, length us, event | category | flops | bytes accessed | tf_op | source)
XLA Modules:
  0.0 317.2 jit_solution(15977437094288833935)
XLA Ops:
  8.0 5.8 %shard_map.73 = bf16[1536,768]{1,0:T(8,128)(2,1)} custom-call(s32[1,1024]{1,0:T(1,128)} %reshape.325.ids_ref, bf16[1024,768]{1,0:T(8,128)(2,1)} %bitcast.55), custom_call_target="tpu_custom_call" | custom-call | tf_op jit(solution)/shard_map/pallas_call | solution.py:64
  13.8 8.7 %all-to-all-start = ((bf16[32,48,768]{2,1,0:T(8,128)(2,1)}), bf16[32,48,768]{2,1,0:T(8,128)(2,1)S(1)}, u32[]{:S(2)}, u32[]{:S(2)}) async-start(bf16[32,48,768]{2,1,0:T(8,128)(2,1)} %bitcast.52), calls=%async_computation | async-start | bytes 4718592 | tf_op jit(solution)/shard_map/all_to_all | solution.py:354
  22.6 3.0 collective-permute-start.4
  25.9 2.4 collective-permute-start.2
  29.5 22.4 %collective-permute-done.4 = f32[16,128]{1,0:T(8,128)S(1)} collective-permute-done((f32[16,128]{1,0:T(8,128)S(1)}, f32[16,128]{1,0:T(8,128)S(1)}, u32[]{:S(2)}, u32[]{:S(2)}) %collective-permute-start.4) | collective-permute-done | bytes 8224 | tf_op jit(solution)/shard_map/ppermute | solution.py:35
  51.9 1.7 all-to-all-done.x_ref
  53.7 1.4 copy-done
  56.5 11.7 %shard_map.74 = bf16[32,48,2048]{2,1,0:T(8,128)(2,1)} custom-call(s32[32]{0:T(128)} %add.310.order_ref, bf16[32,48,768]{2,1,0:T(8,128)(2,1)} %copy-done, bf16[3,768,2048]{2,1,0:T(8,128)(2,1)} %probe_ref.1), custom_call_target="tpu_custom_call" | custom-call | flops 4831838208 | bytes 18087936 | tf_op jit(solution)/shard_map/pallas_call | solution.py:98
  68.3 6.1 %all-to-all-start.1 = ((bf16[8,4,48,2048]{3,2,1,0:T(8,128)(2,1)}), bf16[8,4,48,2048]{3,2,1,0:T(8,128)(2,1)}, u32[]{:S(2)}, u32[]{:S(2)}) async-start(bf16[8,4,48,2048]{3,2,1,0:T(8,128)(2,1)} %bitcast.49), calls=%async_computation.1 | async-start | bytes 12582912 | tf_op jit(solution)/shard_map/all_to_all | solution.py:368
  76.0 10.9 %shard_map.75 = (bf16[4,48,2048]{2,1,0:T(8,128)(2,1)}, bf16[4,48,2048]{2,1,0:T(8,128)(2,1)}, bf16[4,48,2048]{2,1,0:T(8,128)(2,1)}, bf16[4,48,2048]{2,1,0:T(8,128...) custom-call(s32[32]{0:T(128)} %add.341.order_ref, ...), custom_call_target="tpu_custom_call" | custom-call | flops 4831838208 | bytes 18087936 | tf_op jit(solution)/shard_map/pallas_call | solution.py:98
  87.5 3.9 %collective-permute-start.9 = (bf16[4,48,2048]{2,1,0:T(8,128)(2,1)}, bf16[4,48,2048]{2,1,0:T(8,128)(2,1)}, u32[]{:S(2)}, u32[]{:S(2)}) collective-permute-start(bf16[4,48,2048]{2,1,0:T(8,128)(2,1)} %get-tuple-element.59), channel_id=1, source_target_pairs={{0,4},{1,5},{2,6},{3,7},{4,0},{5,1},{6,2},{7,3},{8,12},{9,13},{10,... | collective-permute-start | bytes 2359304 | tf_op jit(solution)/shard_map/ppermute | solution.py:35
  92.1 2.1 collective-permute-start.11
  94.2 13.1 %collective-permute-done.7.refs_2_ = bf16[4,48,2048]{2,1,0:T(8,128)(2,1)S(1)} collective-permute-done((bf16[4,48,2048]{2,1,0:T(8,128)(2,1)}, bf16[4,48,2048]{2,1,0:T(8,128)(2,1)S(1)}, u32[]{:S(2)}, u32[]{:S(2)}) %collective-permute-start.7) | collective-permute-done | bytes 786464 | tf_op jit(solution)/shard_map/ppermute | solution.py:35
  110.6 47.8 %collective-permute-done.8.refs_3_ = bf16[4,48,2048]{2,1,0:T(8,128)(2,1)} collective-permute-done((bf16[4,48,2048]{2,1,0:T(8,128)(2,1)}, bf16[4,48,2048]{2,1,0:T(8,128)(2,1)}, u32[]{:S(2)}, u32[]{:S(2)}) %collective-permute-start.8) | collective-permute-done | bytes 786464 | tf_op jit(solution)/shard_map/ppermute | solution.py:35
  158.4 1.2 collective-permute-done.12.refs_7_
  159.6 9.9 %shard_map.76 = (bf16[4,128,2048]{2,1,0:T(8,128)(2,1)}, f32[128,2048]{1,0:T(8,128)}, bf16[128,2048]{1,0:T(8,128)(2,1)}, bf16[128,2048]{1,0:T(8,128)(2,1)}, bf16[128,2048]{1,0:T(8,128)(2,1)}) custom-call(s32[2,4,24,128]{3,2,1,0:T(8,128)} %bitcast.63, f32[2,4,24,128]{3,2,1,0:T(8,128)} %bitcast.58, bf16[8,4,48,2048]{3,2,1,0:T(8,128)(2,1)} %all-to-all-done.1.tangent_ref, ...), custom_call_target="tpu_custom_call" | custom-call | flops 3221225472 | bytes 12582912 | tf_op jit(solution)/shard_map/pallas_call | solution.py:163
  169.5 4.4 %all-to-all-start.2 = ((bf16[4,128,2048]{2,1,0:T(8,128)(2,1)}), bf16[4,128,2048]{2,1,0:T(8,128)(2,1)}, u32[]{:S(2)}, u32[]{:S(2)}) async-start(bf16[4,128,2048]{2,1,0:T(8,128)(2,1)} %get-tuple-element.76), calls=%async_computation.2 | async-start | bytes 4194304 | tf_op jit(solution)/shard_map/all_to_all | solution.py:406
  174.0 1.5 collective-permute-start.13
  175.5 2.4 collective-permute-start.14
  177.9 1.2 collective-permute-start.15
  179.1 12.6 %shard_map.77.hidden_ref = bf16[4,3,768,512]{3,2,1,0:T(8,128)(2,1)} custom-call(bf16[4,32,48,768]{3,2,1,0:T(8,128)(2,1)} %bitcast.51), custom_call_target="tpu_custom_call" | custom-call | bytes 18874368 | tf_op jit(solution)/shard_map/pallas_call | solution.py:238
  191.7 8.5 %all-to-all-done.2.refs_4_ = bf16[4,128,2048]{2,1,0:T(8,128)(2,1)} async-done(((bf16[4,128,2048]{2,1,0:T(8,128)(2,1)}), bf16[4,128,2048]{2,1,0:T(8,128)(2,1)}, u32[]{:S(2)}, u32[]{:S(2)}) %all-to-all-start.2) | async-done | bytes 2097184 | tf_op jit(solution)/shard_map/all_to_all | solution.py:406
  202.2 4.7 %shard_map.78 = (bf16[128,512]{1,0:T(8,128)(2,1)}, bf16[128,512]{1,0:T(8,128)(2,1)}, bf16[128,512]{1,0:T(8,128)(2,1)}, bf16[128,512]{1,0:T(8,128)(2,1)}) custom-call(s32[1]{0:T(128)} %bitcast.part_ref, f32[128,2048]{1,0:T(8,128)} %get-tuple-element.72.refs_0_, bf16[128,2048]{1,0:T(8,128)(2,1)} %copy-done.3, bf16[128,2048]{1,0:T(8,128)(2,1)} %copy-done.4, ...), custom_call_target="tpu_custom_call" | custom-call | tf_op jit(solution)/shard_map/pallas_call | solution.py:216
  206.9 1.8 collective-permute-start.16
  208.7 3.5 %collective-permute-start.17 = (bf16[128,512]{1,0:T(8,128)(2,1)}, bf16[128,512]{1,0:T(8,128)(2,1)S(1)}, u32[]{:S(2)}, u32[]{:S(2)}) collective-permute-start(bf16[128,512]{1,0:T(8,128)(2,1)} %get-tuple-element.80), channel_id=1, source_target_pairs={{0,64},{32,96},{64,0},{96,32},{1,65},{33,97},{65,1},{97,33},{2,66}... | collective-permute-start | bytes 393224 | tf_op jit(solution)/shard_map/ppermute | solution.py:413
  212.8 1.2 collective-permute-done.16
  214.0 3.4 %collective-permute-done.17 = bf16[128,512]{1,0:T(8,128)(2,1)S(1)} collective-permute-done((bf16[128,512]{1,0:T(8,128)(2,1)}, bf16[128,512]{1,0:T(8,128)(2,1)S(1)}, u32[]{:S(2)}, u32[]{:S(2)}) %collective-permute-start.17) | collective-permute-done | bytes 131104 | tf_op jit(solution)/shard_map/ppermute | solution.py:413
  217.6 1.8 pad_maximum_fusion
  219.4 38.0 %all-gather.1 = bf16[3072,128]{1,0:T(8,128)(2,1)S(1)} all-gather(bf16[24,128]{1,0:T(8,128)(2,1)S(1)} %maximum_bitcast_fusion), channel_id=3, replica_groups=mesh['dp'=4,'expert'=32] {'dp','expert'}, dimensions={0}, use_global_device_ids=true | all-gather | bytes 792576 | tf_op jit(solution)/shard_map/all_gather | solution.py:420
  259.4 1.5 fusion
  261.0 32.8 %all-gather.8.cloned.1.call-done = bf16[128,128,512]{2,1,0:T(8,128)(2,1)} async-done(((bf16[4,128,512]{2,1,0:T(8,128)(2,1)}), bf16[128,128,512]{2,1,0:T(8,128)(2,1)}) %all-gather.8.cloned.1.call-update) | async-done | bytes 16777232 | tf_op jit(solution)/shard_map/all_gather | solution.py:419
  293.7 16.7 %shard_map.79 = f32[3,768,512]{2,1,0:T(8,128)} custom-call(s32[1]{0:T(128)} %bitcast.part_ref, s32[4,32,3,128]{3,2,1,0:T(4,128)} %bitcast.57, f32[4,32,3,128]{3,2,1,0:T(4,128)} %bitcast.56, bf16[4,3,768,512]{3,2,1,0:T(8,128)(2,1)} %shard_map.77.hidden_ref, bf16[32,4,128,512]{3,2,1,0:T(8,128)(2,1)} %bitcast.50, bf16[3,768,2048]{2,1,0:T(8,128)(2,1)} %probe_ref.1), custom_call_target="tpu_custom_call" | custom-call | flops 4831838208 | bytes 33292288 | tf_op jit(solution)/shard_map/pallas_call | solution.py:300
  (98 shorter events, 15.4 us)
Async XLA Ops:
  13.8 8.8 %copy-start.6 = (f32[128,8]{0,1:T(8,128)S(1)}, f32[128,8]{0,1:T(8,128)}, u32[]{:S(2)}) copy-start(f32[128,8]{0,1:T(8,128)} %param.11) | copy-start | bytes 12292
  13.8 8.8 %copy-start.7 = (s32[128,8]{0,1:T(8,128)S(1)}, s32[128,8]{0,1:T(8,128)}, u32[]{:S(2)}) copy-start(s32[128,8]{0,1:T(8,128)} %param.10) | copy-start | bytes 12292
  13.8 39.9 %all-to-all-start = ((bf16[32,48,768]{2,1,0:T(8,128)(2,1)}), bf16[32,48,768]{2,1,0:T(8,128)(2,1)S(1)}, u32[]{:S(2)}, u32[]{:S(2)}) async-start(bf16[32,48,768]{2,1,0:T(8,128)(2,1)} %bitcast.52), calls=%async_computation | async-start | bytes 4718592 | tf_op jit(solution)/shard_map/all_to_all | solution.py:354
  22.5 156.6 %all-gather.6.cloned.1.call-start = ((), (), s32[]{:S(2)}) async-start(), calls=%async_computation.3 | async-start | bytes 11796480 | tf_op jit(solution)/shard_map/all_gather | solution.py:386
  22.6 29.3 %collective-permute-start.4 = (f32[16,128]{1,0:T(8,128)S(1)}, f32[16,128]{1,0:T(8,128)S(1)}, u32[]{:S(2)}, u32[]{:S(2)}) collective-permute-start(f32[16,128]{1,0:T(8,128)S(1)} %pad_maximum_fusion.1), channel_id=1, source_target_pairs={{0,16},{1,17},{2,18},{3,19},{4,20},{5,21},{6,22},{7,23},{8,24},{9,... | collective-permute-start | bytes 24584 | tf_op jit(solution)/shard_map/ppermute | solution.py:35
  25.6 26.3 %collective-permute-start.3 = (f32[16,128]{1,0:T(8,128)S(1)}, f32[16,128]{1,0:T(8,128)S(1)}, u32[]{:S(2)}, u32[]{:S(2)}) collective-permute-start(f32[16,128]{1,0:T(8,128)S(1)} %pad_maximum_fusion.1), channel_id=1, source_target_pairs={{0,8},{1,9},{2,10},{3,11},{4,12},{5,13},{6,14},{7,15},{8,16},{9,17... | collective-permute-start | bytes 24584 | tf_op jit(solution)/shard_map/ppermute | solution.py:35
  25.9 26.0 %collective-permute-start.2 = (f32[16,128]{1,0:T(8,128)S(1)}, f32[16,128]{1,0:T(8,128)S(1)}, u32[]{:S(2)}, u32[]{:S(2)}) collective-permute-start(f32[16,128]{1,0:T(8,128)S(1)} %pad_maximum_fusion.1), channel_id=1, source_target_pairs={{0,6},{1,7},{2,0},{3,1},{4,2},{5,3},{6,4},{7,5},{8,14},{9,15},{10,... | collective-permute-start | bytes 24584 | tf_op jit(solution)/shard_map/ppermute | solution.py:35
  28.4 23.6 %collective-permute-start.1 = (f32[16,128]{1,0:T(8,128)S(1)}, f32[16,128]{1,0:T(8,128)S(1)}, u32[]{:S(2)}, u32[]{:S(2)}) collective-permute-start(f32[16,128]{1,0:T(8,128)S(1)} %pad_maximum_fusion.1), channel_id=1, source_target_pairs={{0,4},{1,5},{2,6},{3,7},{4,0},{5,1},{6,2},{7,3},{8,12},{9,13},{10,... | collective-permute-start | bytes 24584 | tf_op jit(solution)/shard_map/ppermute | solution.py:35
  28.9 23.0 %collective-permute-start = (f32[16,128]{1,0:T(8,128)S(1)}, f32[16,128]{1,0:T(8,128)S(1)}, u32[]{:S(2)}, u32[]{:S(2)}) collective-permute-start(f32[16,128]{1,0:T(8,128)S(1)} %pad_maximum_fusion.1), channel_id=1, source_target_pairs={{0,2},{1,3},{2,4},{3,5},{4,6},{5,7},{6,0},{7,1},{8,10},{9,11},{10,... | collective-permute-start | bytes 24584 | tf_op jit(solution)/shard_map/ppermute | solution.py:35
  53.6 1.4 copy-start
  55.1 13.2 %collective-permute-start.5 = (f32[16,128]{1,0:T(8,128)S(1)}, f32[16,128]{1,0:T(8,128)S(1)}, u32[]{:S(2)}, u32[]{:S(2)}) collective-permute-start(f32[16,128]{1,0:T(8,128)S(1)} %pad_maximum_fusion.1), channel_id=1, source_target_pairs={{0,24},{1,25},{2,26},{3,27},{4,28},{5,29},{6,30},{7,31},{8,0},{9,1... | collective-permute-start | bytes 24584 | tf_op jit(solution)/shard_map/ppermute | solution.py:35
  68.3 91.3 %all-to-all-start.1 = ((bf16[8,4,48,2048]{3,2,1,0:T(8,128)(2,1)}), bf16[8,4,48,2048]{3,2,1,0:T(8,128)(2,1)}, u32[]{:S(2)}, u32[]{:S(2)}) async-start(bf16[8,4,48,2048]{3,2,1,0:T(8,128)(2,1)} %bitcast.49), calls=%async_computation.1 | async-start | bytes 12582912 | tf_op jit(solution)/shard_map/all_to_all | solution.py:368
  86.9 5.2 %collective-permute-start.6 = (bf16[4,48,2048]{2,1,0:T(8,128)(2,1)}, bf16[4,48,2048]{2,1,0:T(8,128)(2,1)S(1)}, u32[]{:S(2)}, u32[]{:S(2)}) collective-permute-start(bf16[4,48,2048]{2,1,0:T(8,128)(2,1)} %get-tuple-element.56), channel_id=1, source_target_pairs={{0,1},{1,0},{2,3},{3,2},{4,5},{5,4},{6,7},{7,6},{8,9},{9,8},{10,11... | collective-permute-start | bytes 2359304 | tf_op jit(solution)/shard_map/ppermute | solution.py:35
  87.1 20.3 %collective-permute-start.7 = (bf16[4,48,2048]{2,1,0:T(8,128)(2,1)}, bf16[4,48,2048]{2,1,0:T(8,128)(2,1)S(1)}, u32[]{:S(2)}, u32[]{:S(2)}) collective-permute-start(bf16[4,48,2048]{2,1,0:T(8,128)(2,1)} %get-tuple-element.57), channel_id=1, source_target_pairs={{0,2},{1,3},{2,4},{3,5},{4,6},{5,7},{6,0},{7,1},{8,10},{9,11},{10,... | collective-permute-start | bytes 2359304 | tf_op jit(solution)/shard_map/ppermute | solution.py:35
  87.2 71.3 %collective-permute-start.8 = (bf16[4,48,2048]{2,1,0:T(8,128)(2,1)}, bf16[4,48,2048]{2,1,0:T(8,128)(2,1)}, u32[]{:S(2)}, u32[]{:S(2)}) collective-permute-start(bf16[4,48,2048]{2,1,0:T(8,128)(2,1)} %get-tuple-element.58), channel_id=1, source_target_pairs={{0,3},{1,2},{2,5},{3,4},{4,7},{5,6},{6,1},{7,0},{8,11},{9,10},{10,... | collective-permute-start | bytes 2359304 | tf_op jit(solution)/shard_map/ppermute | solution.py:35
  87.5 70.9 %collective-permute-start.9 = (bf16[4,48,2048]{2,1,0:T(8,128)(2,1)}, bf16[4,48,2048]{2,1,0:T(8,128)(2,1)}, u32[]{:S(2)}, u32[]{:S(2)}) collective-permute-start(bf16[4,48,2048]{2,1,0:T(8,128)(2,1)} %get-tuple-element.59), channel_id=1, source_target_pairs={{0,4},{1,5},{2,6},{3,7},{4,0},{5,1},{6,2},{7,3},{8,12},{9,13},{10,... | collective-permute-start | bytes 2359304 | tf_op jit(solution)/shard_map/ppermute | solution.py:35
  91.4 67.0 %collective-permute-start.10 = (bf16[4,48,2048]{2,1,0:T(8,128)(2,1)}, bf16[4,48,2048]{2,1,0:T(8,128)(2,1)}, u32[]{:S(2)}, u32[]{:S(2)}) collective-permute-start(bf16[4,48,2048]{2,1,0:T(8,128)(2,1)} %get-tuple-element.60), channel_id=1, source_target_pairs={{0,5},{1,4},{2,7},{3,6},{4,1},{5,0},{6,3},{7,2},{8,13},{9,12},{10,... | collective-permute-start | bytes 2359304 | tf_op jit(solution)/shard_map/ppermute | solution.py:35
  92.1 67.5 %copy-start.1 = (bf16[4,48,2048]{2,1,0:T(8,128)(2,1)}, bf16[4,48,2048]{2,1,0:T(8,128)(2,1)S(1)}, u32[]{:S(2)}) copy-start(bf16[4,48,2048]{2,1,0:T(8,128)(2,1)S(1)} %collective-permute-done.6.refs_1_) | copy-start | bytes 2359300
  92.1 66.3 %collective-permute-start.11 = (bf16[4,48,2048]{2,1,0:T(8,128)(2,1)}, bf16[4,48,2048]{2,1,0:T(8,128)(2,1)}, u32[]{:S(2)}, u32[]{:S(2)}) collective-permute-start(bf16[4,48,2048]{2,1,0:T(8,128)(2,1)} %get-tuple-element.61), channel_id=1, source_target_pairs={{0,6},{1,7},{2,0},{3,1},{4,2},{5,3},{6,4},{7,5},{8,14},{9,15},{10,... | collective-permute-start | bytes 2359304 | tf_op jit(solution)/shard_map/ppermute | solution.py:35
  107.4 52.3 %copy-start.2 = (bf16[4,48,2048]{2,1,0:T(8,128)(2,1)}, bf16[4,48,2048]{2,1,0:T(8,128)(2,1)S(1)}, u32[]{:S(2)}) copy-start(bf16[4,48,2048]{2,1,0:T(8,128)(2,1)S(1)} %collective-permute-done.7.refs_2_) | copy-start | bytes 2359300
  107.4 52.2 %collective-permute-start.12 = (bf16[4,48,2048]{2,1,0:T(8,128)(2,1)}, bf16[4,48,2048]{2,1,0:T(8,128)(2,1)}, u32[]{:S(2)}, u32[]{:S(2)}) collective-permute-start(bf16[4,48,2048]{2,1,0:T(8,128)(2,1)} %get-tuple-element.62), channel_id=1, source_target_pairs={{0,7},{1,6},{2,1},{3,0},{4,3},{5,2},{6,5},{7,4},{8,15},{9,14},{10,... | collective-permute-start | bytes 2359304 | tf_op jit(solution)/shard_map/ppermute | solution.py:35
  169.5 30.7 %all-to-all-start.2 = ((bf16[4,128,2048]{2,1,0:T(8,128)(2,1)}), bf16[4,128,2048]{2,1,0:T(8,128)(2,1)}, u32[]{:S(2)}, u32[]{:S(2)}) async-start(bf16[4,128,2048]{2,1,0:T(8,128)(2,1)} %get-tuple-element.76), calls=%async_computation.2 | async-start | bytes 4194304 | tf_op jit(solution)/shard_map/all_to_all | solution.py:406
  173.9 119.8 %all-gather.8.cloned.1.call-start = ((), (), s32[]{:S(2)}) async-start(), calls=%async_computation.4 | async-start | bytes 17301504 | tf_op jit(solution)/shard_map/all_gather | solution.py:419
  174.0 26.2 %collective-permute-start.13 = (bf16[128,2048]{1,0:T(8,128)(2,1)}, bf16[128,2048]{1,0:T(8,128)(2,1)S(1)}, u32[]{:S(2)}, u32[]{:S(2)}) collective-permute-start(bf16[128,2048]{1,0:T(8,128)(2,1)} %get-tuple-element.73), channel_id=1, source_target_pairs={{0,8},{1,9},{2,10},{3,11},{4,12},{5,13},{6,14},{7,15},{8,16},{9,17... | collective-permute-start | bytes 1572872 | tf_op jit(solution)/shard_map/ppermute | solution.py:35
  175.5 25.7 %collective-permute-start.14 = (bf16[128,2048]{1,0:T(8,128)(2,1)}, bf16[128,2048]{1,0:T(8,128)(2,1)S(1)}, u32[]{:S(2)}, u32[]{:S(2)}) collective-permute-start(bf16[128,2048]{1,0:T(8,128)(2,1)} %get-tuple-element.74), channel_id=1, source_target_pairs={{0,16},{1,17},{2,18},{3,19},{4,20},{5,21},{6,22},{7,23},{8,24},{9,... | collective-permute-start | bytes 1572872 | tf_op jit(solution)/shard_map/ppermute | solution.py:35
  177.9 23.3 %collective-permute-start.15 = (bf16[128,2048]{1,0:T(8,128)(2,1)}, bf16[128,2048]{1,0:T(8,128)(2,1)S(1)}, u32[]{:S(2)}, u32[]{:S(2)}) collective-permute-start(bf16[128,2048]{1,0:T(8,128)(2,1)} %get-tuple-element.75), channel_id=1, source_target_pairs={{0,24},{1,25},{2,26},{3,27},{4,28},{5,29},{6,30},{7,31},{8,0},{9,1... | collective-permute-start | bytes 1572872 | tf_op jit(solution)/shard_map/ppermute | solution.py:35
  200.2 1.0 copy-start.3
  201.2 0.8 copy-start.4
  201.2 1.0 copy-start.5
  206.9 7.1 %collective-permute-start.16 = (bf16[128,512]{1,0:T(8,128)(2,1)}, bf16[128,512]{1,0:T(8,128)(2,1)S(1)}, u32[]{:S(2)}, u32[]{:S(2)}) collective-permute-start(bf16[128,512]{1,0:T(8,128)(2,1)} %get-tuple-element.79), channel_id=1, source_target_pairs={{0,32},{32,64},{64,96},{96,0},{1,33},{33,65},{65,97},{97,1},{2,34}... | collective-permute-start | bytes 393224 | tf_op jit(solution)/shard_map/ppermute | solution.py:413
  208.7 8.7 %collective-permute-start.17 = (bf16[128,512]{1,0:T(8,128)(2,1)}, bf16[128,512]{1,0:T(8,128)(2,1)S(1)}, u32[]{:S(2)}, u32[]{:S(2)}) collective-permute-start(bf16[128,512]{1,0:T(8,128)(2,1)} %get-tuple-element.80), channel_id=1, source_target_pairs={{0,64},{32,96},{64,0},{96,32},{1,65},{33,97},{65,1},{97,33},{2,66}... | collective-permute-start | bytes 393224 | tf_op jit(solution)/shard_map/ppermute | solution.py:413
  212.2 5.5 %collective-permute-start.18 = (bf16[128,512]{1,0:T(8,128)(2,1)}, bf16[128,512]{1,0:T(8,128)(2,1)S(1)}, u32[]{:S(2)}, u32[]{:S(2)}) collective-permute-start(bf16[128,512]{1,0:T(8,128)(2,1)} %get-tuple-element.81), channel_id=1, source_target_pairs={{0,96},{32,0},{64,32},{96,64},{1,97},{33,1},{65,33},{97,65},{2,98}... | collective-permute-start | bytes 393224 | tf_op jit(solution)/shard_map/ppermute | solution.py:413
Sparse Core Ops, SparseCore 0:
  55.2 90.9 all-gather.5
  219.6 74.1 all-gather.7
